TPU v7x, 32 devices: a whole 2x2x4 slice. The times are simulated.
32 devices in a mesh: seq: 8 (over y, x, core), hid: 4 (over z).
Axes of the slice: x: 2, y: 2, z: 4, core: 2. Of those that a mesh axis runs over, the one named last changes fastest.
Arguments:
- tokens_in: bfloat16 [32, 1024, 768], P('hid', 'seq'), may hold values from -6 to 6
- image_lengths: int32 [32, 64], P('hid'), may hold values from 0 to 1024, as said below
- attn_weight: float32 [3072, 768], P('hid')
- attn_moment: float32 [3072, 768], P('hid'), may hold values from -512 to 512
- attn_average: float32 [3072, 768], P('hid')
- mlp_weight: float32 [2, 3072, 768], P(None, 'hid'), may hold values from -0.21875 to 0.21875
- mlp_moment: float32 [2, 3072, 768], P(None, 'hid'), may hold values from -512 to 512
- mlp_average: float32 [2, 3072, 768], P(None, 'hid'), may hold values from -0.21875 to 0.21875
- vector_params: float32 [12, 768], replicated
- vector_moment: float32 [12, 768], replicated, may hold values from -512 to 512
- vector_average: float32 [12, 768], replicated
- out_grad: bfloat16 [32, 1024, 768], P('hid', 'seq'), may hold values from -6 to 6
Outputs:
- block_out: float32 [32, 1024, 768], P('hid', 'seq')
- input_grad: float32 [32, 1024, 768], P('hid', 'seq')
- attn_grad: float32 [3072, 768], P('hid')
- attn_moment_new: float32 [3072, 768], P('hid')
- attn_weight_new: float32 [3072, 768], P('hid')
- attn_average_new: float32 [3072, 768], P('hid')
- mlp_grad: float32 [2, 3072, 768], P(None, 'hid')
- mlp_moment_new: float32 [2, 3072, 768], P(None, 'hid')
- mlp_weight_new: float32 [2, 3072, 768], P(None, 'hid')
- mlp_average_new: float32 [2, 3072, 768], P(None, 'hid')
- vector_grad: float32 [12, 768], replicated
- vector_moment_new: float32 [12, 768], replicated
- vector_params_new: float32 [12, 768], replicated
- vector_average_new: float32 [12, 768], replicated
Inputs may be any that keep to these rules, and one draw needn't show every extreme that they name: `image_lengths`: the nonzero entries of a row come first; a row sums to between 897 and 1024, and the positions after its sum are padding. Among the 8 rows of each index of hid, one holds a single image of 1024 patches.
All inputs are finite; a program needn't handle non-finite values.
Results may differ from a plain program's by a relative error of at most 0.019.
Values may be sent and summed in bfloat16 or wider, within the bound.
No kernel may reach another device: no remote copies, remote signals or barrier semaphores. Data moves between devices by JAX's collectives and lax.ppermute only.
A program may use at most 320 MiB of HBM per device.

v0:
```python
import jax
import jax.numpy as jnp
from jax import lax
from jax.sharding import PartitionSpec as P

HEADS = 12
HEAD_DIM = 64
FF = 3072


score_scale = 0.125
norm_eps = 1e-06
big_negative = -1e30
matrix_rate = 0.0001
vector_rate = 0.001
momentum_decay = 0.9
weight_decay = 0.0001
average_decay = 0.9


def segment_of(image_lengths, positions):
    image_ends = jnp.cumsum(image_lengths, axis=1)
    return jnp.sum((image_ends[:, None, :] <= positions[None, :, None]).astype(jnp.int32), axis=2)


def normalize(inputs, gain_row, offset):
    center = inputs - jnp.mean(inputs, axis=-1, keepdims=True)
    spread = jnp.mean(center * center, axis=-1, keepdims=True)
    return center * lax.rsqrt(spread + norm_eps) * gain_row + offset


def gelu_exact(inputs):
    return jax.nn.gelu(inputs, approximate=False)


def masked_scores(query_heads, key_heads, query_segments, key_segments):
    scores = (
        jnp.einsum("bqhd,bkhd->bqhk", query_heads, key_heads, preferred_element_type=jnp.float32)
        * score_scale
    )
    same_image = query_segments[:, :, None, None] == key_segments[:, None, None, :]
    return jnp.where(same_image, scores, big_negative)


def renew(weight, moment, average, gradient, decay_rate, step_rate):
    step_grad = gradient + decay_rate * weight
    moment_new = momentum_decay * moment + step_grad
    weight_new = weight - step_rate * (step_grad + momentum_decay * moment_new)
    average_new = average_decay * average + (1.0 - average_decay) * weight_new
    return (gradient, moment_new, weight_new, average_new)


def shards(
    tokens_in,
    image_lengths,
    attn_weight,
    attn_moment,
    attn_average,
    mlp_weight,
    mlp_moment,
    mlp_average,
    vector_params,
    vector_moment,
    vector_average,
    out_grad,
):
    pack_count, row_count, model_width = tokens_in.shape
    token_count = pack_count * row_count
    seq_index = lax.axis_index("seq")
    hid_index = lax.axis_index("hid")
    query_positions = seq_index * row_count + jnp.arange(row_count, dtype=jnp.int32)
    query_segments = segment_of(image_lengths, query_positions)
    used_total = jnp.sum(image_lengths, axis=1)
    query_valid = (query_positions[None, :] < used_total[:, None]).astype(jnp.float32)
    gathered_attn = lax.all_gather(attn_weight.astype(jnp.bfloat16), "hid", axis=0, tiled=True)
    w_qkv = gathered_attn[: 3 * model_width]
    w_out = gathered_attn[3 * model_width :]
    gain_one, shift_one, bias_query, bias_value, bias_out, gain_two, shift_two, bias_down = [
        vector_params[row_index] for row_index in range(8)
    ]
    hidden_bias = vector_params[8:].reshape(-1)
    tokens_wide = tokens_in.astype(jnp.float32)
    first_norm, first_back = jax.vjp(normalize, tokens_wide, gain_one, shift_one)
    first_low = first_norm.astype(jnp.bfloat16)
    first_flat = first_low.reshape(token_count, model_width)
    projected = jnp.einsum(
        "td,ed->te", first_flat, w_qkv, preferred_element_type=jnp.float32
    ).reshape(pack_count, row_count, 3 * model_width)
    head_shape = (pack_count, row_count, HEADS, HEAD_DIM)
    queries = (projected[..., :model_width] + bias_query).astype(jnp.bfloat16)
    keys_low = projected[..., model_width : 2 * model_width].astype(jnp.bfloat16)
    values_low = (projected[..., 2 * model_width :] + bias_value).astype(jnp.bfloat16)
    query_heads = queries.reshape(head_shape)
    stat_shape = (pack_count, row_count, HEADS)
    running_max = jnp.full(stat_shape, big_negative, jnp.float32)
    key_block = lax.all_gather(keys_low, "seq", axis=1, tiled=True)
    value_block = lax.all_gather(values_low, "seq", axis=1, tiled=True)
    block_rows = key_block.shape[1]
    block_shape = (pack_count, block_rows, HEADS, HEAD_DIM)
    key_segments = segment_of(image_lengths, jnp.arange(block_rows, dtype=jnp.int32))
    scores = masked_scores(
        query_heads, key_block.reshape(block_shape), query_segments, key_segments
    )
    new_max = jnp.maximum(running_max, jnp.max(scores, axis=-1))
    weights = jnp.exp(scores - new_max[..., None])
    new_sum = jnp.sum(weights, axis=-1)
    update = jnp.einsum(
        "bqhk,bkhd->bqhd",
        weights.astype(jnp.bfloat16),
        value_block.reshape(block_shape),
        preferred_element_type=jnp.float32,
    )
    attended = update / new_sum[..., None]
    log_total = new_max + jnp.log(new_sum)
    mixed_low = (attended.reshape(tokens_in.shape) * query_valid[..., None]).astype(jnp.bfloat16)
    mixed_flat = mixed_low.reshape(token_count, model_width)
    branch_out = (
        jnp.einsum("td,ed->te", mixed_flat, w_out, preferred_element_type=jnp.float32).reshape(
            tokens_in.shape
        )
        + bias_out
    )
    residual = tokens_wide + branch_out
    second_norm, second_back = jax.vjp(normalize, residual, gain_two, shift_two)
    second_low = second_norm.astype(jnp.bfloat16)
    hidden_count = mlp_weight.shape[1]
    w_up = mlp_weight[0].astype(jnp.bfloat16)
    w_down = mlp_weight[1].astype(jnp.bfloat16)
    bias_piece = lax.dynamic_slice_in_dim(hidden_bias, hid_index * hidden_count, hidden_count)
    group_inputs = lax.all_gather(second_low, "hid", axis=0, tiled=True)
    group_flat = group_inputs.reshape(-1, model_width)
    group_active = gelu_exact(
        jnp.einsum("td,fd->tf", group_flat, w_up, preferred_element_type=jnp.float32) + bias_piece
    ).astype(jnp.bfloat16)
    group_terms = jnp.einsum(
        "tf,fd->td", group_active, w_down, preferred_element_type=jnp.float32
    ).reshape(group_inputs.shape)
    mlp_out = lax.psum_scatter(
        group_terms.astype(jnp.bfloat16), "hid", scatter_dimension=0, tiled=True
    ).astype(jnp.float32)
    block_out = residual + mlp_out + bias_down
    grad_wide = out_grad.astype(jnp.float32)
    grad_down_bias = jnp.sum(grad_wide, axis=(0, 1))
    input_piece = lax.all_gather(second_low, "hid", axis=0, tiled=True)
    piece_packs = input_piece.shape[0]
    flat_input = input_piece.reshape(-1, model_width)
    flat_grad = lax.all_gather(out_grad, "hid", axis=0, tiled=True).reshape(-1, model_width)
    before = (
        jnp.einsum("td,fd->tf", flat_input, w_up, preferred_element_type=jnp.float32) + bias_piece
    )
    active, active_back = jax.vjp(gelu_exact, before)
    grad_active = jnp.einsum("td,fd->tf", flat_grad, w_down, preferred_element_type=jnp.float32)
    grad_before = active_back(grad_active)[0].astype(jnp.bfloat16)
    up_grad = jnp.einsum("tf,td->fd", grad_before, flat_input, preferred_element_type=jnp.float32)
    down_grad = jnp.einsum(
        "tf,td->fd", active.astype(jnp.bfloat16), flat_grad, preferred_element_type=jnp.float32
    )
    bias_grad = jnp.sum(grad_before.astype(jnp.float32), axis=0)
    piece_grads = jnp.einsum(
        "tf,fd->td", grad_before, w_up, preferred_element_type=jnp.float32
    ).reshape(piece_packs, row_count, model_width)
    second_grad = lax.psum_scatter(
        piece_grads.astype(jnp.bfloat16), "hid", scatter_dimension=0, tiled=True
    ).astype(jnp.float32)
    mlp_grad_part = jnp.stack([up_grad, down_grad])
    bias_grad_full = lax.dynamic_update_slice_in_dim(
        jnp.zeros((FF,), jnp.float32), bias_grad, hid_index * hidden_count, 0
    )
    residual_part, grad_gain_two, grad_shift_two = second_back(second_grad)
    residual_grad = grad_wide + residual_part
    branch_grad = residual_grad.astype(jnp.bfloat16)
    grad_bias_out = jnp.sum(branch_grad.astype(jnp.float32), axis=(0, 1))
    branch_flat = branch_grad.reshape(token_count, model_width)
    grad_w_out = jnp.einsum(
        "te,td->ed", branch_flat, mixed_flat, preferred_element_type=jnp.float32
    )
    mixed_grad = jnp.einsum(
        "te,ed->td", branch_flat, w_out, preferred_element_type=jnp.float32
    ).reshape(tokens_in.shape)
    mixed_grad = mixed_grad.astype(jnp.bfloat16) * query_valid[..., None].astype(jnp.bfloat16)
    grad_heads = mixed_grad.reshape(head_shape)
    row_delta = jnp.sum(grad_heads.astype(jnp.float32) * attended, axis=-1)
    key_block = lax.all_gather(keys_low, "seq", axis=1, tiled=True)
    value_block = lax.all_gather(values_low, "seq", axis=1, tiled=True)
    block_rows = key_block.shape[1]
    block_shape = (pack_count, block_rows, HEADS, HEAD_DIM)
    key_heads = key_block.reshape(block_shape)
    key_segments = segment_of(image_lengths, jnp.arange(block_rows, dtype=jnp.int32))
    scores = masked_scores(query_heads, key_heads, query_segments, key_segments)
    probs = jnp.exp(scores - log_total[..., None])
    prob_grad = jnp.einsum(
        "bqhd,bkhd->bqhk",
        grad_heads,
        value_block.reshape(block_shape),
        preferred_element_type=jnp.float32,
    )
    score_grad = (probs * (prob_grad - row_delta[..., None])).astype(jnp.bfloat16)
    probs, score_grad = (probs, score_grad)
    value_part = jnp.einsum(
        "bqhk,bqhd->bkhd",
        probs.astype(jnp.bfloat16),
        grad_heads,
        preferred_element_type=jnp.float32,
    )
    query_grad = (
        jnp.einsum("bqhk,bkhd->bqhd", score_grad, key_heads, preferred_element_type=jnp.float32)
        * score_scale
    )
    key_part = (
        jnp.einsum("bqhk,bqhd->bkhd", score_grad, query_heads, preferred_element_type=jnp.float32)
        * score_scale
    )
    key_grads = key_part.reshape(pack_count, block_rows, model_width)
    value_grads = value_part.reshape(pack_count, block_rows, model_width)
    back_result = (query_grad, key_grads, value_grads)
    query_grad = back_result[0]
    key_grad, value_grad = (
        lax.psum_scatter(
            back_result[1].astype(jnp.bfloat16), "seq", scatter_dimension=1, tiled=True
        ).astype(jnp.float32),
        lax.psum_scatter(
            back_result[2].astype(jnp.bfloat16), "seq", scatter_dimension=1, tiled=True
        ).astype(jnp.float32),
    )
    query_grad_low = query_grad.reshape(tokens_in.shape).astype(jnp.bfloat16)
    key_grad_low = key_grad.astype(jnp.bfloat16)
    value_grad_low = value_grad.astype(jnp.bfloat16)
    joined_grad = jnp.concatenate([query_grad_low, key_grad_low, value_grad_low], axis=-1).reshape(
        token_count, 3 * model_width
    )
    grad_w_qkv = jnp.einsum(
        "te,td->ed", joined_grad, first_flat, preferred_element_type=jnp.float32
    )
    grad_bias_query = jnp.sum(query_grad_low.astype(jnp.float32), axis=(0, 1))
    grad_bias_value = jnp.sum(value_grad_low.astype(jnp.float32), axis=(0, 1))
    first_grad = jnp.einsum(
        "te,ed->td", joined_grad, w_qkv, preferred_element_type=jnp.float32
    ).reshape(tokens_in.shape)
    input_part, grad_gain_one, grad_shift_one = first_back(first_grad)
    input_grad = residual_grad + input_part
    vector_rows_grad = jnp.stack(
        [
            grad_gain_one,
            grad_shift_one,
            grad_bias_query,
            grad_bias_value,
            grad_bias_out,
            grad_gain_two,
            grad_shift_two,
            grad_down_bias,
        ]
    )
    vector_part = jnp.concatenate(
        [vector_rows_grad, bias_grad_full.reshape(-1, model_width)], axis=0
    )
    vector_part = lax.psum(vector_part.astype(jnp.bfloat16), "hid").astype(jnp.float32)
    attn_part = lax.psum_scatter(
        jnp.concatenate([grad_w_qkv, grad_w_out], axis=0).astype(jnp.bfloat16),
        "hid",
        scatter_dimension=0,
        tiled=True,
    )
    attn_grad, mlp_grad, vector_grad = (
        lax.psum(attn_part, "seq").astype(jnp.float32),
        lax.psum(mlp_grad_part.astype(jnp.bfloat16), "seq").astype(jnp.float32),
        lax.psum(vector_part.astype(jnp.bfloat16), "seq").astype(jnp.float32),
    )
    attn_new = renew(attn_weight, attn_moment, attn_average, attn_grad, weight_decay, matrix_rate)
    mlp_new = renew(mlp_weight, mlp_moment, mlp_average, mlp_grad, weight_decay, matrix_rate)
    vector_new = renew(vector_params, vector_moment, vector_average, vector_grad, 0.0, vector_rate)
    return (
        block_out,
        input_grad,
        attn_new[0],
        attn_new[1],
        attn_new[2],
        attn_new[3],
        mlp_new[0],
        mlp_new[1],
        mlp_new[2],
        mlp_new[3],
        vector_new[0],
        vector_new[1],
        vector_new[2],
        vector_new[3],
    )


def solution(mesh):
    return jax.shard_map(
        shards,
        mesh=mesh,
        in_specs=(
            P("hid", "seq", None),
            P("hid", None),
            P("hid", None),
            P("hid", None),
            P("hid", None),
            P(None, "hid", None),
            P(None, "hid", None),
            P(None, "hid", None),
            P(),
            P(),
            P(),
            P("hid", "seq", None),
        ),
        out_specs=(
            P("hid", "seq", None),
            P("hid", "seq", None),
            P("hid", None),
            P("hid", None),
            P("hid", None),
            P("hid", None),
            P(None, "hid", None),
            P(None, "hid", None),
            P(None, "hid", None),
            P(None, "hid", None),
            P(),
            P(),
            P(),
            P(),
        ),
        check_vma=False,
    )
```

profile of v0, /device:TPU:9, one launch (start us, length us, event | category | flops | bytes accessed | tf_op | source)
XLA Modules:
  0.0 1229.4 jit_solution(3218931514595978678)
XLA Ops:
  7.2 2.9 convert_element_type.162
  11.8 86.5 %all-gather.6.cloned.1.call-done = bf16[3072,768]{1,0:T(8,128)(2,1)} async-done(((bf16[768,768]{1,0:T(8,128)(2,1)}), bf16[3072,768]{1,0:T(8,128)(2,1)}) %all-gather.6.cloned.1.call-update) | async-done | bytes 4718608 | tf_op jit(solution)/shard_map/all_gather | solution.py:75
  98.3 6.1 fusion.42
  104.5 3.6 copy-done.13
  109.5 5.2 fusion.39
  118.1 2.4 copy.73
  120.5 62.7 %all-gather.10.cloned.1.call-done = bf16[8,1024,768]{2,1,0:T(8,128)(2,1)} async-done(((bf16[8,128,768]{2,1,0:T(8,128)(2,1)}), bf16[8,1024,768]{2,1,0:T(8,128)(2,1)}) %all-gather.10.cloned.1.call-update) | async-done | bytes 12582928 | tf_op jit(solution)/shard_map/all_gather | solution.py:96
  183.2 16.8 %copy.72 = bf16[8,1024,768]{1,2,0:T(8,128)(2,1)} copy(bf16[8,1024,768]{2,1,0:T(8,128)(2,1)} %all-gather.10.cloned.1.call-done) | data formatting | bytes 25165824 | tf_op jit(solution)/shard_map/all_gather | solution.py:96
  200.0 25.1 %fusion.5 = (f32[8,128,12]{1,2,0:T(8,128)S(1)}, f32[8,12,1024,128]{3,2,1,0:T(8,128)}) fusion(pred[8,128,1024]{1,2,0:T(8,128)(4,1)S(1)} %broadcast_compare_fusion, bf16[8,1024,12,64]{1,3,2,0:T(8,128)(2,1)} %bitcast.102, bf16[8,128,12,64]{1,3,2,0:T(8,128)(2,1)S(1)} %bitcast.105), kind=kOutput, calls=%fused_computation.9 | convolution fusion | flops 1648349184 | bytes 65585152 | tf_op jit(solution)/shard_map/bqhd,bkhd->bqhk/dot_general | solution.py:38
  225.8 21.3 %fusion.2 = f32[8,128,12]{1,2,0:T(8,128)S(1)} fusion(f32[8,12,1024,128]{3,2,1,0:T(8,128)} %get-tuple-element.55, f32[8,128,12]{1,2,0:T(8,128)S(1)} %broadcast_maximum_fusion, pred[8,128,1024]{1,2,0:T(8,128)(4,1)S(1)} %broadcast_compare_fusion), kind=kLoop, calls=%fused_computation.6 | loop fusion | flops 50319360 | bytes 51478528 | tf_op jit(solution)/shard_map/reduce_sum | solution.py:106
  247.1 10.8 all-gather.8.cloned.1.call-done
  257.9 16.6 %copy.71 = bf16[8,1024,768]{1,2,0:T(8,128)(2,1)} copy(bf16[8,1024,768]{2,1,0:T(8,128)(2,1)} %all-gather.8.cloned.1.call-done) | data formatting | bytes 25165824 | tf_op jit(solution)/shard_map/all_gather | solution.py:97
  274.5 22.7 %bitcast_divide_fusion = f32[8,128,12,64]{1,3,2,0:T(8,128)S(1)} fusion(bf16[8,1024,12,64]{1,3,2,0:T(8,128)(2,1)} %bitcast.107, f32[8,12,1024,128]{3,2,1,0:T(8,128)} %get-tuple-element.55, f32[8,128,12]{1,2,0:T(8,128)S(1)} %broadcast_maximum_fusion, pred[8,128,1024]{1,2,0:T(8,128)(4,1)} %copy-done.10, f32[8,128,12]{1,2,0:T(8,128)S(1)} %fusion.2), kind=kOutput, calls=%fused_computation.74 | convolution fusion | flops 1661730816 | bytes 67207168 | tf_op jit(solution)/shard_map/bqhk,bkhd->bqhd/dot_general | solution.py:107
  297.2 2.7 copy.75
  299.9 4.3 fusion.78
  307.1 4.0 convert.58
  311.1 107.5 %all-gather.12.cloned.1.call-done = bf16[32,128,768]{2,1,0:T(8,128)(2,1)} async-done(((bf16[8,128,768]{2,1,0:T(8,128)(2,1)}), bf16[32,128,768]{2,1,0:T(8,128)(2,1)}) %all-gather.12.cloned.1.call-update) | async-done | bytes 6291472 | tf_op jit(solution)/shard_map/all_gather | solution.py:130
  418.7 35.2 %multiply_convert_fusion.1 = (bf16[4096,768]{1,0:T(8,128)(2,1)}, f32[4096,768]{1,0:T(8,128)}, f32[4096,768]{1,0:T(8,128)}) fusion(f32[768]{0:T(1024)S(1)} %dynamic_slice.3, bf16[4096,768]{1,0:T(8,128)(2,1)} %bitcast.115, bf16[2,768,768]{2,1,0:T(8,128)(2,1)} %convert.58), kind=kOutput, calls=%fused_computation.22 | convolution fusion | flops 5039456256 | bytes 38931456 | tf_op jit(solution)/shard_map/td,fd->tf/dot_general | solution.py:133
  453.9 79.8 %all-gather.14.cloned.1.call-done = bf16[32,128,768]{2,1,0:T(8,128)(2,1)} async-done(((bf16[8,128,768]{2,1,0:T(8,128)(2,1)}), bf16[32,128,768]{2,1,0:T(8,128)(2,1)}) %all-gather.14.cloned.1.call-update) | async-done | bytes 6291472 | tf_op jit(solution)/shard_map/all_gather | solution.py:147
  533.7 18.7 %convert_reduce_fusion = (bf16[768]{0:T(1024)(128)(2,1)S(1)}, bf16[4096,768]{1,0:T(8,128)(2,1)}) fusion(f32[4096,768]{1,0:T(8,128)} %get-tuple-element.45, bf16[4096,768]{1,0:T(8,128)(2,1)} %bitcast.117, bf16[2,768,768]{2,1,0:T(8,128)(2,1)} %convert.58, f32[4096,768]{1,0:T(8,128)} %get-tuple-element.58, f32[768]{0:T(1024)S(1)} %dynamic_slice.3), kind=kOutput, calls=%fused_computation.20 | convolution fusion | flops 4885314560 | bytes 38932992 | tf_op jit(solution)/shard_map/td,fd->tf/dot_general | solution.py:152
  552.4 9.6 convolution_convert_fusion
  562.9 111.2 %reduce-scatter.8.cloned.1.call-done = bf16[8,128,768]{2,1,0:T(8,128)(2,1)} async-done(((bf16[32,128,768]{2,1,0:T(8,128)(2,1)}), bf16[8,128,768]{2,1,0:T(8,128)(2,1)}) %reduce-scatter.8.cloned.1.call-update) | async-done | bytes 1572880 | tf_op jit(solution)/shard_map/reduce_scatter | solution.py:162
  674.0 2.2 fusion.35
  681.5 3.8 fusion.46
  687.3 24.4 %fusion.21 = bf16[8,12,64,1024]{3,2,1,0:T(8,128)(2,1)} fusion(bf16[8,128,12,64]{1,3,2,0:T(8,128)(2,1)S(1)} %bitcast.112, f32[8,12,1024,128]{3,2,1,0:T(8,128)} %get-tuple-element.55, f32[8,128,12]{1,2,0:T(8,128)S(1)} %log_add_fusion, pred[8,128,1024]{1,2,0:T(8,128)(4,1)S(1)} %copy-done.11), kind=kOutput, calls=%fused_computation.37 | convolution fusion | flops 1667235840 | bytes 65585152 | tf_op jit(solution)/shard_map/bqhk,bqhd->bkhd/dot_general | solution.py:199
  711.7 16.7 %copy.81 = bf16[8,1024,768]{2,1,0:T(8,128)(2,1)} copy(bf16[8,1024,768]{1,2,0:T(8,128)(2,1)} %bitcast.109) | data formatting | bytes 25165824 | tf_op jit(solution)/shard_map/convert_element_type | solution.py:222
  730.3 2.2 multiply_reduce_fusion
  732.6 37.2 %fusion.1 = bf16[8,128,12,1024]{1,3,2,0:T(8,128)(2,1)} fusion(f32[8,12,1024,128]{3,2,1,0:T(8,128)} %get-tuple-element.55, f32[8,128,12]{1,2,0:T(8,128)S(1)} %multiply_reduce_fusion, f32[8,128,12]{1,2,0:T(8,128)S(1)} %log_add_fusion, pred[8,128,1024]{1,2,0:T(8,128)(4,1)S(1)} %copy-done.12, bf16[8,1024,12,64]{1,3,2,0:T(8,128)(2,1)} %bitcast.108, ...), kind=kOutput, calls=%fused_computation.2 | convolution fusion | flops 1686110208 | bytes 90800128 | tf_op jit(solution)/shard_map/bqhd,bkhd->bqhk/dot_general | solution.py:191
  769.8 18.4 %multiply_convert_fusion = bf16[8,12,64,1024]{3,2,1,0:T(8,128)(2,1)} fusion(bf16[8,128,12,64]{1,3,2,0:T(8,128)(2,1)S(1)} %bitcast.106, bf16[8,128,12,1024]{1,3,2,0:T(8,128)(2,1)} %fusion.1), kind=kOutput, calls=%fused_computation.11 | convolution fusion | flops 1623195648 | bytes 39321600 | tf_op jit(solution)/shard_map/bqhk,bqhd->bkhd/dot_general | solution.py:210
  788.1 16.7 %copy.79 = bf16[8,1024,768]{2,1,0:T(8,128)(2,1)} copy(bf16[8,1024,768]{1,2,0:T(8,128)(2,1)} %bitcast.104) | data formatting | bytes 25165824 | tf_op jit(solution)/shard_map/convert_element_type | solution.py:219
  804.9 14.9 %fusion.79 = (bf16[12,64]{1,0:T(8,128)(2,1)S(1)}, bf16[8,12,64,128]{3,2,1,0:T(8,128)(2,1)S(1)}) fusion(bf16[8,1024,12,64]{1,3,2,0:T(8,128)(2,1)} %bitcast.103, bf16[8,128,12,1024]{1,3,2,0:T(8,128)(2,1)} %fusion.1), kind=kOutput, calls=%fused_computation.151 | convolution fusion | flops 1612971264 | bytes 39323136 | tf_op jit(solution)/shard_map/bqhk,bkhd->bqhd/dot_general | solution.py:206
  821.4 4.6 bitcast_convert_fusion.1
  826.0 91.4 %reduce-scatter.10.cloned.1.call-done = bf16[8,128,768]{2,1,0:T(8,128)(2,1)} async-done(((bf16[8,1024,768]{2,1,0:T(8,128)(2,1)}), bf16[8,128,768]{2,1,0:T(8,128)(2,1)}) %reduce-scatter.10.cloned.1.call-update) | async-done | bytes 1572880 | tf_op jit(solution)/shard_map/reduce_scatter | solution.py:218
  917.4 6.5 bitcast_convert_fusion
  923.9 2.5 pad_maximum_fusion.1
  926.5 9.2 convolution_convert_fusion.1
  936.5 9.0 fusion.48
  945.5 9.1 fusion.47
  956.7 8.6 fusion.74
  965.7 46.2 %reduce-scatter.14.cloned.1.call-done = bf16[768,768]{1,0:T(8,128)(2,1)} async-done(((bf16[3072,768]{1,0:T(8,128)(2,1)}), bf16[768,768]{1,0:T(8,128)(2,1)}) %reduce-scatter.14.cloned.1.call-update) | async-done | bytes 1179664 | tf_op jit(solution)/shard_map/reduce_scatter | solution.py:257
  1012.0 3.3 fusion.34
  1015.4 16.0 %psum.30 = bf16[12,768]{1,0:T(8,128)(2,1)S(1)} all-reduce(bf16[12,768]{1,0:T(8,128)(2,1)S(1)} %concatenate.13), channel_id=1, replica_groups=mesh['seq'=8,'hid'=4] {'hid'}, use_global_device_ids=true, to_apply=%region_31.32 | all-reduce | flops 9216 | bytes 36864 | tf_op jit(solution)/shard_map/psum | solution.py:256
  1031.5 25.9 %psum.31 = bf16[12,768]{1,0:T(8,128)(2,1)S(1)} all-reduce(bf16[12,768]{1,0:T(8,128)(2,1)S(1)} %psum.30), channel_id=1, replica_groups=mesh['seq'=8,'hid'=4] {'seq'}, use_global_device_ids=true, to_apply=%region_32.33 | all-reduce | flops 9216 | bytes 36864 | tf_op jit(solution)/shard_map/psum | solution.py:266
  1058.1 68.0 %reduce-scatter.6.cloned.1.call-done = bf16[8,128,768]{2,1,0:T(8,128)(2,1)} async-done(((bf16[32,128,768]{2,1,0:T(8,128)(2,1)}), bf16[8,128,768]{2,1,0:T(8,128)(2,1)}) %reduce-scatter.6.cloned.1.call-update) | async-done | bytes 1572880 | tf_op jit(solution)/shard_map/reduce_scatter | solution.py:138
  1126.1 6.7 add_add_fusion.2
  1132.8 71.7 %all-reduce.3.cloned.1.call-done = (bf16[768,768]{1,0:T(8,128)(2,1)}, bf16[2,768,768]{2,1,0:T(8,128)(2,1)}) async-done(((bf16[768,768]{1,0:T(8,128)(2,1)}, bf16[2,768,768]{2,1,0:T(8,128)(2,1)}), (bf16[768,768]{1,0:T(8,128)(2,1)}, bf16[2,768,768]{2,1,0:T(8,128)(2,1)})) %all-reduce.3.cloned.1.call-update) | async-done | bytes 3538960 | tf_op jit(solution)/shard_map/psum | solution.py:264
  1204.5 7.8 multiply_add_fusion.3
  1212.3 10.4 multiply_add_fusion
  (178 shorter events, 25.4 us)
Async XLA Ops:
  7.2 3.7 copy-start.2
  7.2 91.1 %all-gather.6.cloned.1.call-start = ((), (), s32[]{:S(2)}) async-start(), calls=%async_computation.5 | async-start | bytes 5898240 | tf_op jit(solution)/shard_map/all_gather | solution.py:75
  10.2 173.0 %all-gather.10.cloned.1.call-start = ((), (), s32[]{:S(2)}) async-start(), calls=%async_computation.7 | async-start | bytes 14155776 | tf_op jit(solution)/shard_map/all_gather | solution.py:96
  10.9 93.6 %copy-start.42 = (f32[768]{0:T(1024)}, f32[768]{0:T(1024)S(1)}, u32[]{:S(2)}) copy-start(f32[768]{0:T(1024)S(1)} %get-tuple-element.27) | copy-start | bytes 9220
  10.9 93.6 %copy-start.50 = (f32[768]{0:T(1024)}, f32[768]{0:T(1024)S(1)}, u32[]{:S(2)}) copy-start(f32[768]{0:T(1024)S(1)} %get-tuple-element.26) | copy-start | bytes 9220
  10.9 667.5 %copy-start.30 = (f32[768]{0:T(1024)}, f32[768]{0:T(1024)S(1)}, u32[]{:S(2)}) copy-start(f32[768]{0:T(1024)S(1)} %get-tuple-element.22) | copy-start | bytes 9220
  11.2 93.3 %copy-start.36 = (f32[8,128]{1,0:T(8,128)}, f32[8,128]{1,0:T(8,128)S(1)}, u32[]{:S(2)}) copy-start(f32[8,128]{1,0:T(8,128)S(1)} %broadcast_multiply_fusion.1) | copy-start | bytes 12292
  11.8 92.7 %copy-start.46 = (f32[8,128]{1,0:T(8,128)}, f32[8,128]{1,0:T(8,128)S(1)}, u32[]{:S(2)}) copy-start(f32[8,128]{1,0:T(8,128)S(1)} %fusion.37) | copy-start | bytes 12292
  11.8 92.7 %copy-start.44 = (f32[8,128]{1,0:T(8,128)}, f32[8,128]{1,0:T(8,128)S(1)}, u32[]{:S(2)}) copy-start(f32[8,128]{1,0:T(8,128)S(1)} %fusion.64) | copy-start | bytes 12292
  109.4 148.4 %all-gather.8.cloned.1.call-start = ((), (), s32[]{:S(2)}) async-start(), calls=%async_computation.6 | async-start | bytes 14155776 | tf_op jit(solution)/shard_map/all_gather | solution.py:97
  109.5 5.5 copy-start.49
  114.7 304.0 %all-gather.12.cloned.1.call-start = ((), (), s32[]{:S(2)}) async-start(), calls=%async_computation.8 | async-start | bytes 7864320 | tf_op jit(solution)/shard_map/all_gather | solution.py:130
  116.6 183.2 %copy-start.52 = (f32[8,128]{1,0:T(8,128)}, f32[8,128]{1,0:T(8,128)S(1)}, u32[]{:S(2)}) copy-start(f32[8,128]{1,0:T(8,128)S(1)} %get-tuple-element.53) | copy-start | bytes 12292
  118.1 107.7 %copy-start.10 = (pred[8,128,1024]{1,2,0:T(8,128)(4,1)}, pred[8,128,1024]{1,2,0:T(8,128)(4,1)S(1)}, u32[]{:S(2)}) copy-start(pred[8,128,1024]{1,2,0:T(8,128)(4,1)S(1)} %broadcast_compare_fusion) | copy-start | bytes 3145732
  120.5 79.5 %copy-start.6 = (bf16[8,128,768]{1,2,0:T(8,128)(2,1)}, bf16[8,128,768]{1,2,0:T(8,128)(2,1)S(1)}, u32[]{:S(2)}) copy-start(bf16[8,128,768]{1,2,0:T(8,128)(2,1)S(1)} %copy.73) | copy-start | bytes 4718596
  247.1 27.4 %copy-start.24 = (f32[8,128,12]{1,2,0:T(8,128)}, f32[8,128,12]{1,2,0:T(8,128)S(1)}, u32[]{:S(2)}) copy-start(f32[8,128,12]{1,2,0:T(8,128)S(1)} %fusion.2) | copy-start | bytes 147460
  304.1 374.2 %copy-start = (f32[8,128,768]{2,1,0:T(8,128)}, f32[8,128,768]{2,1,0:T(8,128)S(1)}, u32[]{:S(2)}) copy-start(f32[8,128,768]{2,1,0:T(8,128)S(1)} %get-tuple-element.57) | copy-start | bytes 9437188
  304.2 374.2 %copy-start.26 = (f32[8,128]{1,0:T(8,128)}, f32[8,128]{1,0:T(8,128)S(1)}, u32[]{:S(2)}) copy-start(f32[8,128]{1,0:T(8,128)S(1)} %broadcast_multiply_fusion) | copy-start | bytes 12292
  304.6 373.7 %copy-start.32 = (f32[8,128]{1,0:T(8,128)}, f32[8,128]{1,0:T(8,128)S(1)}, u32[]{:S(2)}) copy-start(f32[8,128]{1,0:T(8,128)S(1)} %fusion.65) | copy-start | bytes 12292
  306.4 227.3 %all-gather.14.cloned.1.call-start = ((), (), s32[]{:S(2)}) async-start(), calls=%async_computation.10 | async-start | bytes 7864320 | tf_op jit(solution)/shard_map/all_gather | solution.py:147
  307.0 367.1 %reduce-scatter.8.cloned.1.call-start = ((), (), s32[]{:S(2)}) async-start(), calls=%async_computation.11 | async-start | bytes 7864320 | tf_op jit(solution)/shard_map/reduce_scatter | solution.py:162
  533.7 18.7 %copy-start.17 = (bf16[2,768,768]{2,1,0:T(8,128)(2,1)S(1)}, bf16[2,768,768]{2,1,0:T(8,128)(2,1)}, u32[]{:S(2)}) copy-start(bf16[2,768,768]{2,1,0:T(8,128)(2,1)} %convert.58) | copy-start | bytes 7077892
  562.0 263.9 %reduce-scatter.12.cloned.1.call-start = ((), (), s32[]{:S(2)}) async-start(), calls=%async_computation.13 | async-start | bytes 14155776 | tf_op jit(solution)/shard_map/reduce_scatter | solution.py:221
  676.3 4.0 copy-start.34
  687.3 24.4 %copy-start.14 = (bf16[8,128,768]{1,2,0:T(8,128)(2,1)}, bf16[8,128,768]{1,2,0:T(8,128)(2,1)S(1)}, u32[]{:S(2)}) copy-start(bf16[8,128,768]{1,2,0:T(8,128)(2,1)S(1)} %copy.76) | copy-start | bytes 4718596
  728.4 189.0 %reduce-scatter.10.cloned.1.call-start = ((), (), s32[]{:S(2)}) async-start(), calls=%async_computation.12 | async-start | bytes 14155776 | tf_op jit(solution)/shard_map/reduce_scatter | solution.py:218
  732.5 37.2 %copy-start.7 = (bf16[8,128,768]{1,2,0:T(8,128)(2,1)S(1)}, bf16[8,128,768]{1,2,0:T(8,128)(2,1)}, u32[]{:S(2)}) copy-start(bf16[8,128,768]{1,2,0:T(8,128)(2,1)} %copy-done.6) | copy-start | bytes 4718596
  804.8 207.1 %reduce-scatter.14.cloned.1.call-start = ((), (), s32[]{:S(2)}) async-start(), calls=%async_computation.14 | async-start | bytes 5898240 | tf_op jit(solution)/shard_map/reduce_scatter | solution.py:257
  821.3 96.0 %copy-start.3 = (bf16[8,128,768]{2,1,0:T(8,128)(2,1)S(1)}, bf16[8,128,768]{2,1,0:T(8,128)(2,1)}, u32[]{:S(2)}) copy-start(bf16[8,128,768]{2,1,0:T(8,128)(2,1)} %param.12) | copy-start | bytes 4718596
  821.3 96.0 %copy-start.37 = (f32[8,128]{1,0:T(8,128)S(1)}, f32[8,128]{1,0:T(8,128)}, u32[]{:S(2)}) copy-start(f32[8,128]{1,0:T(8,128)} %copy-done.36) | copy-start | bytes 12292
  821.4 96.0 %copy-start.43 = (f32[768]{0:T(1024)S(1)}, f32[768]{0:T(1024)}, u32[]{:S(2)}) copy-start(f32[768]{0:T(1024)} %copy-done.42) | copy-start | bytes 9220
  821.4 96.0 %copy-start.45 = (f32[8,128]{1,0:T(8,128)S(1)}, f32[8,128]{1,0:T(8,128)}, u32[]{:S(2)}) copy-start(f32[8,128]{1,0:T(8,128)} %copy-done.44) | copy-start | bytes 12292
  821.4 96.0 %copy-start.51 = (f32[768]{0:T(1024)S(1)}, f32[768]{0:T(1024)}, u32[]{:S(2)}) copy-start(f32[768]{0:T(1024)} %copy-done.50) | copy-start | bytes 9220
  826.0 98.0 %copy-start.21 = (bf16[768,768]{1,0:T(8,128)(2,1)S(1)}, bf16[768,768]{1,0:T(8,128)(2,1)}, u32[]{:S(2)}) copy-start(bf16[768,768]{1,0:T(8,128)(2,1)} %bitcast_convert_fusion.1) | copy-start | bytes 3538948
  926.4 199.6 %reduce-scatter.6.cloned.1.call-start = ((), (), s32[]{:S(2)}) async-start(), calls=%async_computation.9 | async-start | bytes 7864320 | tf_op jit(solution)/shard_map/reduce_scatter | solution.py:138
  935.7 268.7 %all-reduce.3.cloned.1.call-start = ((), (), s32[]{:S(2)}) async-start(), calls=%async_computation.15 | async-start | bytes 7077888 | tf_op jit(solution)/shard_map/psum | solution.py:264
  956.7 8.9 copy-start.47
  1011.9 45.5 %copy-start.29 = (f32[12,768]{1,0:T(8,128)S(1)}, f32[12,768]{1,0:T(8,128)}, u32[]{:S(2)}) copy-start(f32[12,768]{1,0:T(8,128)} %param.20) | copy-start | bytes 110596
  1011.9 45.4 %copy-start.38 = (f32[12,768]{1,0:T(8,128)S(1)}, f32[12,768]{1,0:T(8,128)}, u32[]{:S(2)}) copy-start(f32[12,768]{1,0:T(8,128)} %param.22) | copy-start | bytes 110596
  1011.9 45.4 %copy-start.39 = (f32[12,768]{1,0:T(8,128)S(1)}, f32[12,768]{1,0:T(8,128)}, u32[]{:S(2)}) copy-start(f32[12,768]{1,0:T(8,128)} %param.21) | copy-start | bytes 110596
  1012.0 114.1 %copy-start.1 = (f32[8,128,768]{2,1,0:T(8,128)S(1)}, f32[8,128,768]{2,1,0:T(8,128)}, u32[]{:S(2)}) copy-start(f32[8,128,768]{2,1,0:T(8,128)} %copy-done) | copy-start | bytes 9437188
  1012.0 114.1 %copy-start.27 = (f32[8,128]{1,0:T(8,128)S(1)}, f32[8,128]{1,0:T(8,128)}, u32[]{:S(2)}) copy-start(f32[8,128]{1,0:T(8,128)} %copy-done.26) | copy-start | bytes 12292
  1012.0 114.1 %copy-start.31 = (f32[768]{0:T(1024)S(1)}, f32[768]{0:T(1024)}, u32[]{:S(2)}) copy-start(f32[768]{0:T(1024)} %copy-done.30) | copy-start | bytes 9220
  1012.0 114.1 %copy-start.33 = (f32[8,128]{1,0:T(8,128)S(1)}, f32[8,128]{1,0:T(8,128)}, u32[]{:S(2)}) copy-start(f32[8,128]{1,0:T(8,128)} %copy-done.32) | copy-start | bytes 12292
  1012.0 114.1 %copy-start.35 = (f32[8,128]{1,0:T(8,128)S(1)}, f32[8,128]{1,0:T(8,128)}, u32[]{:S(2)}) copy-start(f32[8,128]{1,0:T(8,128)} %copy-done.34) | copy-start | bytes 12292
  1012.0 114.1 %copy-start.41 = (f32[8,128]{1,0:T(8,128)S(1)}, f32[8,128]{1,0:T(8,128)}, u32[]{:S(2)}) copy-start(f32[8,128]{1,0:T(8,128)} %copy-done.40) | copy-start | bytes 12292
  1012.0 114.1 %copy-start.48 = (f32[768]{0:T(1024)S(1)}, f32[768]{0:T(1024)}, u32[]{:S(2)}) copy-start(f32[768]{0:T(1024)} %get-tuple-element.20) | copy-start | bytes 9220
  1204.5 7.8 copy-start.16
  (19 other events, 38.3 us)
Sparse Core Ops, SparseCore 0:
  10.3 87.9 all-gather.5
  109.6 73.5 all-gather.9
  185.7 72.1 all-gather.7
  306.5 112.0 all-gather.11
  420.1 113.5 all-gather.13
  562.1 111.8 reduce-scatter.7
  728.5 92.8 reduce-scatter.11
  824.9 92.3 reduce-scatter.9
  926.6 85.2 reduce-scatter.13
  1014.0 111.9 reduce-scatter.5
  1130.0 74.3 all-reduce.2
where the time goes:
time: 1240 us; the launch traced here: 1230 us
  waiting for transfers between devices  737 us (59%)
  matrix products  267 us (22%)
  local copies, waits for them, and re-layouts  86.9 us (7%)
  other arithmetic  81 us (7%)
  blocking collectives  41.9 us (3%)
  between operations  14.9 us (1%)
    reduce_scatter x1, waiting for transfers between devices, shards(): lax.psum_scatter(piece_grads.astype(jnp.bfloat16), 'hid', scatter_dimensi...  111 us
    all_gather x1, waiting for transfers between devices, shards(): group_inputs = lax.all_gather(second_low, 'hid', axis=0, tiled=True)  108 us
    reduce_scatter x1, waiting for transfers between devices, shards(): lax.psum_scatter(back_result[1].astype(jnp.bfloat16), 'seq', scatter_dime...  91.4 us
    all_gather x1, waiting for transfers between devices, shards(): lax.all_gather(attn_weight.astype(jnp.bfloat16), 'hid', axis=0, tiled=True)  86.5 us
    all_gather x1, waiting for transfers between devices, shards(): lax.all_gather(out_grad, 'hid', axis=0, tiled=True).reshape(-1, model_width)  79.8 us
    psum x1, waiting for transfers between devices, shards(): lax.psum(attn_part, 'seq').astype(jnp.float32)  71.7 us
    reduce_scatter x1, waiting for transfers between devices, shards(): lax.psum_scatter(group_terms.astype(jnp.bfloat16), 'hid', scatter_dimensi...  68 us
    all_gather x1, waiting for transfers between devices, shards(): key_block = lax.all_gather(keys_low, 'seq', axis=1, tiled=True)  62.7 us
  transfers between devices with their start and end apart: 11, of which 10 were waited for; matrix products, arithmetic and copies ran while one was open for 21% of the time, Pallas kernels for 0%

commit v1 on v0

v1 whole, which is shorter than its diff:
```python
import functools

import jax
import jax.numpy as jnp
from jax import lax
from jax.experimental import pallas as pl
from jax.experimental.pallas import tpu as pltpu
from jax.sharding import PartitionSpec as P

HEADS = 12
HEAD_DIM = 64

score_scale = 0.125
norm_eps = 1e-06
big_negative = -1e30
matrix_rate = 0.0001
vector_rate = 0.001
momentum_decay = 0.9
weight_decay = 0.0001
average_decay = 0.9

low = jnp.bfloat16
wide = jnp.float32
kernel_vmem = 56 * 1024 * 1024


def rows_by_rows(a, b):
    return lax.dot_general(a, b, (((1,), (1,)), ((), ())), preferred_element_type=wide)


def rows_by_cols(a, b):
    return lax.dot_general(a, b, (((1,), (0,)), ((), ())), preferred_element_type=wide)


def cols_by_cols(a, b):
    return lax.dot_general(a, b, (((0,), (0,)), ((), ())), preferred_element_type=wide)


def normalize(inputs, gain_row, offset):
    center = inputs - jnp.mean(inputs, axis=-1, keepdims=True)
    spread = jnp.mean(center * center, axis=-1, keepdims=True)
    return center * lax.rsqrt(spread + norm_eps) * gain_row + offset


def renew(weight, moment, average, gradient, decay_rate, step_rate):
    step_grad = gradient + decay_rate * weight
    moment_new = momentum_decay * moment + step_grad
    weight_new = weight - step_rate * (step_grad + momentum_decay * moment_new)
    average_new = average_decay * average + (1.0 - average_decay) * weight_new
    return (gradient, moment_new, weight_new, average_new)


def params(**kwargs):
    return pltpu.CompilerParams(vmem_limit_bytes=kernel_vmem, **kwargs)


def smem():
    return pl.BlockSpec(memory_space=pltpu.SMEM)


def whole_vmem():
    return pl.BlockSpec(memory_space=pltpu.VMEM)


def attention_forward_kernel(
    tile, q_ref, k_ref, v_ref, query_seg, key_seg, valid_ref, o_ref, lse_ref
):
    rows = q_ref.shape[0]
    lane = lax.broadcasted_iota(jnp.int32, (1, 128), 1)
    k = k_ref[...]
    v = v_ref[...]
    v_and_ones = jnp.concatenate([v, jnp.ones_like(v)], axis=1)
    for start in range(0, rows, tile):
        part = pl.ds(start, tile)
        q = q_ref[part, :]
        same = query_seg[part, :] == key_seg[...]
        heads = []
        for head in range(2):
            mine = (lane // HEAD_DIM) == head
            scores = rows_by_rows(jnp.where(mine, q, jnp.zeros_like(q)), k)
            scores = jnp.where(same, scores, big_negative)
            top = jnp.max(scores, axis=1, keepdims=True)
            weights = jnp.exp(scores - top).astype(low)
            sums = rows_by_cols(weights, v_and_ones)
            total = sums[:, 128:]
            heads.append(sums[:, :128] / total)
            lse_ref[0, head : head + 1, part] = jnp.transpose(top + jnp.log(total))[:1, :]
        joined = jnp.where(lane < HEAD_DIM, heads[0], heads[1]) * valid_ref[part, :]
        o_ref[part, :] = joined.astype(low)


def attention_forward(q, k, v, query_seg, key_seg, valid):
    rows, width = q.shape
    keys = k.shape[0]
    pairs = width // 128
    column = lambda n: pl.BlockSpec((n, 128), lambda g: (0, g))
    whole = lambda a: pl.BlockSpec(a.shape, lambda g: (0, 0))
    return pl.pallas_call(
        functools.partial(attention_forward_kernel, min(128, rows)),
        grid=(pairs,),
        in_specs=[
            column(rows),
            column(keys),
            column(keys),
            whole(query_seg),
            whole(key_seg),
            whole(valid),
        ],
        out_specs=[column(rows), pl.BlockSpec((1, 2, rows), lambda g: (g, 0, 0))],
        out_shape=[
            jax.ShapeDtypeStruct((rows, width), low),
            jax.ShapeDtypeStruct((pairs, 2, rows), wide),
        ],
        compiler_params=params(),
        cost_estimate=pl.CostEstimate(
            flops=20 * rows * keys * width,
            bytes_accessed=8 * rows * width,
            transcendentals=rows * keys * pairs * 2,
        ),
        name="attention_forward",
    )(q, k, v, query_seg, key_seg, valid)


def attention_backward_kernel(
    tile,
    q_ref,
    k_ref,
    v_ref,
    do_ref,
    lse_ref,
    delta_ref,
    query_seg,
    key_seg,
    dq_ref,
    dk_ref,
    dv_ref,
    dk_sum,
    dv_sum,
):
    rows = q_ref.shape[0]
    lane = lax.broadcasted_iota(jnp.int32, (1, 128), 1)
    k = k_ref[...]
    v = v_ref[...]
    for start in range(0, rows, tile):
        part = pl.ds(start, tile)
        q = q_ref[part, :]
        do = do_ref[part, :]
        same = key_seg[...] == query_seg[:, part]
        heads = []
        dk = 0.0
        dv = 0.0
        for head in range(2):
            mine = (lane // HEAD_DIM) == head
            q_head = jnp.where(mine, q, jnp.zeros_like(q))
            do_head = jnp.where(mine, do, jnp.zeros_like(do))
            scores = jnp.where(same, rows_by_rows(k, q_head), big_negative)
            probs = jnp.exp(scores - lse_ref[0, head : head + 1, part])
            grads = rows_by_rows(v, do_head)
            grads = (probs * (grads - delta_ref[0, head : head + 1, part])).astype(low)
            dv = dv + rows_by_cols(probs.astype(low), do_head)
            dk = dk + rows_by_cols(grads, q_head)
            heads.append(cols_by_cols(grads, k))
        joined = jnp.where(lane < HEAD_DIM, heads[0], heads[1])
        dq_ref[part, :] = (score_scale * joined).astype(low)
        if start == 0:
            dk_sum[...] = dk
            dv_sum[...] = dv
        else:
            dk_sum[...] += dk
            dv_sum[...] += dv
    dk_ref[...] = dk_sum[...].astype(low)
    dv_ref[...] = dv_sum[...].astype(low)


def attention_backward(q, k, v, do, lse, delta, query_seg, key_seg):
    rows, width = q.shape
    keys = k.shape[0]
    pairs = width // 128
    column = lambda n: pl.BlockSpec((n, 128), lambda g: (0, g))
    whole = lambda a: pl.BlockSpec(a.shape, lambda g: (0, 0))
    stat = pl.BlockSpec((1, 2, rows), lambda g: (g, 0, 0))
    return pl.pallas_call(
        functools.partial(attention_backward_kernel, min(256, rows)),
        grid=(pairs,),
        in_specs=[
            column(rows),
            column(keys),
            column(keys),
            column(rows),
            stat,
            stat,
            whole(query_seg),
            whole(key_seg),
        ],
        out_specs=[column(rows), column(keys), column(keys)],
        out_shape=[
            jax.ShapeDtypeStruct((rows, width), low),
            jax.ShapeDtypeStruct((keys, width), low),
            jax.ShapeDtypeStruct((keys, width), low),
        ],
        scratch_shapes=[pltpu.VMEM((keys, 128), wide), pltpu.VMEM((keys, 128), wide)],
        compiler_params=params(),
        cost_estimate=pl.CostEstimate(
            flops=40 * rows * keys * width,
            bytes_accessed=14 * rows * width,
            transcendentals=rows * keys * pairs * 2,
        ),
        name="attention_backward",
    )(q, k, v, do, lse, delta, query_seg, key_seg)


def mlp_step(a, dy, up, down, bias):
    before = rows_by_rows(a, up) + bias
    grad_active = rows_by_rows(dy, down)
    density = 0.3989422804014327 * jnp.exp(-0.5 * before * before)
    below = 0.5 * (1.0 + lax.erf(before * 0.7071067811865476))
    active = (before * below).astype(low)
    grad_before = ((below + before * density) * grad_active).astype(low)
    bias_grad = jnp.sum(grad_before.astype(wide), axis=0, keepdims=True)
    up_grad = cols_by_cols(grad_before, a)
    down_grad = cols_by_cols(active, dy)
    return (
        rows_by_cols(active, down),
        rows_by_cols(grad_before, up),
        up_grad,
        down_grad,
        bias_grad,
    )


def add_up(step, steps, out_ref, da_ref, out_sum, da_sum, out_term, da_term):
    @pl.when(step == 0)
    def _():
        out_sum[...] = out_term
        da_sum[...] = da_term

    @pl.when(step > 0)
    def _():
        out_sum[...] += out_term
        da_sum[...] += da_term

    @pl.when(step == steps - 1)
    def _():
        out_ref[...] = out_sum[...]
        da_ref[...] = da_sum[...]


def mlp_plain_kernel(
    a_ref, dy_ref, up_ref, dn_ref, hb_ref, out_ref, da_ref, gup, gdn, ghb, out_sum, da_sum
):
    out_term, da_term, up_grad, down_grad, bias_grad = mlp_step(
        a_ref[...], dy_ref[...], up_ref[...], dn_ref[...], hb_ref[0]
    )
    gup[...] = up_grad.astype(low)
    gdn[...] = down_grad.astype(low)
    ghb[0] = bias_grad
    add_up(
        pl.program_id(0), pl.num_programs(0), out_ref, da_ref, out_sum, da_sum, out_term, da_term
    )


def mlp_plain(a, dy, up, down, bias, step_width=768):
    rows, width = a.shape
    hidden = up.shape[0]
    steps = hidden // step_width
    whole = pl.BlockSpec((rows, width), lambda i: (0, 0))
    chunk = pl.BlockSpec((step_width, width), lambda i: (i, 0))
    strip = pl.BlockSpec((1, 1, step_width), lambda i: (i, 0, 0))
    return pl.pallas_call(
        mlp_plain_kernel,
        grid=(steps,),
        in_specs=[whole, whole, chunk, chunk, strip],
        out_specs=[whole, whole, chunk, chunk, strip],
        out_shape=[jax.ShapeDtypeStruct((rows, width), wide)] * 2
        + [jax.ShapeDtypeStruct((hidden, width), low)] * 2
        + [jax.ShapeDtypeStruct((steps, 1, step_width), wide)],
        scratch_shapes=[pltpu.VMEM((rows, width), wide)] * 2,
        compiler_params=params(),
        name="mlp_both_ways",
    )(a, dy, up, down, bias.reshape(steps, 1, step_width))


def mlp_pieces_kernel(
    halves,
    place,
    a_ref,
    dy_ref,
    local_ref,
    *refs,
):
    even_refs = refs[:halves]
    odd_ref, hb_ref, out_ref, da_ref, even_grad, odd_grad, ghb, out_sum, da_sum, up, down = refs[
        halves:
    ]
    step = pl.program_id(0)
    seq_index = place[1]
    count = 2 * halves
    piece = even_refs[0].shape[2]

    @pl.when(step == 0)
    def _():
        for other in range(count):
            source = pl.ds(pl.multiple_of((seq_index ^ other) * piece, 16), piece)
            target = pl.ds(other * piece, piece)
            up[target, :] = local_ref[0, source, :]
            down[target, :] = local_ref[1, source, :]

    @pl.when(step > 0)
    def _():
        for other in range(count):
            target = pl.ds(other * piece, piece)
            if other % 2 == 0:
                up[target, :] = even_refs[other // 2][0, 0]
                down[target, :] = even_refs[other // 2][0, 1]
            else:
                up[target, :] = odd_ref[other // 2, 0, 0]
                down[target, :] = odd_ref[other // 2, 0, 1]

    out_term, da_term, up_grad, down_grad, bias_grad = mlp_step(
        a_ref[...], dy_ref[...], up[...], down[...], hb_ref[0]
    )
    up_grad = up_grad.astype(low)
    down_grad = down_grad.astype(low)
    for other in range(count):
        target = even_grad if other % 2 == 0 else odd_grad
        target[other // 2, 0, 0] = up_grad[other * piece : (other + 1) * piece, :]
        target[other // 2, 0, 1] = down_grad[other * piece : (other + 1) * piece, :]
    ghb[0] = bias_grad
    add_up(step, pl.num_programs(0), out_ref, da_ref, out_sum, da_sum, out_term, da_term)


def mlp_pieces(place, a, dy, local, evens, odds, bias):
    rows, width = a.shape
    halves = len(evens)
    steps, _, piece, _ = evens[0].shape
    steps += 1
    step_width = 2 * halves * piece
    whole = pl.BlockSpec((rows, width), lambda i, p: (0, 0))
    strip = pl.BlockSpec((1, 1, step_width), lambda i, p: (i, 0, 0))
    grads = pl.BlockSpec((halves, 1, 2, piece, width), lambda i, p: (0, i, 0, 0, 0))
    before = lambda i: jnp.maximum(i - 1, 0)
    return pl.pallas_call(
        functools.partial(mlp_pieces_kernel, halves),
        grid_spec=pltpu.PrefetchScalarGridSpec(
            num_scalar_prefetch=1,
            grid=(steps,),
            in_specs=[whole, whole, pl.BlockSpec(local.shape, lambda i, p: (0, 0, 0))]
            + [pl.BlockSpec((1, 2, piece, width), lambda i, p: (before(i), 0, 0, 0))] * halves
            + [
                pl.BlockSpec(
                    (halves, 1, 2, piece, width), lambda i, p: (0, before(i), 0, 0, 0)
                ),
                strip,
            ],
            out_specs=[whole, whole, grads, grads, strip],
            scratch_shapes=[pltpu.VMEM((rows, width), wide)] * 2
            + [pltpu.VMEM((step_width, width), low)] * 2,
        ),
        out_shape=[jax.ShapeDtypeStruct((rows, width), wide)] * 2
        + [jax.ShapeDtypeStruct((halves, steps, 2, piece, width), low)] * 2
        + [jax.ShapeDtypeStruct((steps, 1, step_width), wide)],
        compiler_params=params(),
        cost_estimate=pl.CostEstimate(
            flops=12 * rows * steps * step_width * width,
            bytes_accessed=24 * rows * width,
            transcendentals=rows * steps * step_width * 2,
        ),
        name="mlp_both_ways",
    )(place, a, dy, local, *evens, odds, bias)


def assemble_kernel(halves, place, local_ref, *refs):
    even_refs = refs[:halves]
    odd_ref, out_ref = refs[halves:]
    hid_index, seq_index = place[0], place[1]
    quarter = local_ref.shape[0]
    others, piece, _ = even_refs[0].shape
    out_ref[pl.ds(pl.multiple_of(hid_index * quarter, 16), quarter), :] = local_ref[...]
    for step in range(others):
        for other in range(2 * halves):
            start = (hid_index ^ (step + 1)) * quarter + (seq_index ^ other) * piece
            target = pl.ds(pl.multiple_of(start, 16), piece)
            if other % 2 == 0:
                out_ref[target, :] = even_refs[other // 2][step]
            else:
                out_ref[target, :] = odd_ref[other // 2, step]


def assemble(place, local, evens, odds):
    quarter, width = local.shape
    halves = len(evens)
    groups = evens[0].shape[0] + 1
    return pl.pallas_call(
        functools.partial(assemble_kernel, halves),
        in_specs=[smem()] + [whole_vmem()] * (halves + 2),
        out_specs=whole_vmem(),
        out_shape=jax.ShapeDtypeStruct((groups * quarter, width), low),
        compiler_params=params(),
        name="assemble_rows",
    )(place, local, *evens, odds)


def place_packs_kernel(place, own_ref, *refs):
    out_ref = refs[-1]
    packs = out_ref.shape[0]
    seq_index = place[1]
    out_ref[seq_index % packs] = own_ref[...]
    for other in range(1, packs):
        out_ref[(seq_index ^ other) % packs] = refs[other - 1][...].astype(wide)


def place_packs(place, own, others):
    rows, width = own.shape
    packs = len(others) + 1
    return pl.pallas_call(
        place_packs_kernel,
        in_specs=[smem()] + [whole_vmem()] * packs,
        out_specs=whole_vmem(),
        out_shape=jax.ShapeDtypeStruct((packs, rows, width), wide),
        compiler_params=params(),
        name="place_packs",
    )(place, own, *others)


def matrix_grads_kernel(seqs, place, dq, dk, dv, dt, a_ref, o_ref, out_ref):
    hid_index, seq_index = place[0], place[1]
    _, _, piece, width = out_ref.shape
    for matrix, (rows, other) in enumerate(((dq, a_ref), (dk, a_ref), (dv, a_ref), (dt, o_ref))):
        grad = cols_by_cols(rows[...], other[...]).astype(low)
        for chunk in range(width // piece):
            number = matrix * (width // piece) + chunk
            step = (number // seqs) ^ hid_index
            away = (number % seqs) ^ seq_index
            slot = (away % 2) * (seqs // 2) + away // 2
            out_ref[slot, step] = grad[chunk * piece : (chunk + 1) * piece, :]


def matrix_grads(place, seqs, hids, dq, dk, dv, dt, a, o):
    width = a.shape[1]
    piece = 4 * width // (seqs * hids)
    return pl.pallas_call(
        functools.partial(matrix_grads_kernel, seqs),
        in_specs=[smem()] + [whole_vmem()] * 6,
        out_specs=whole_vmem(),
        out_shape=jax.ShapeDtypeStruct((seqs, hids, piece, width), low),
        compiler_params=params(),
        cost_estimate=pl.CostEstimate(
            flops=8 * a.shape[0] * width * width,
            bytes_accessed=12 * a.shape[0] * width,
            transcendentals=0,
        ),
        name="matrix_grads",
    )(place, dq, dk, dv, dt, a, o)


def renew_kernel(place, grads, weight, moment, average, *outs):
    source = place[1] ^ pl.program_id(0)
    gradient = grads[source].astype(wide)
    results = renew(
        weight[...], moment[...], average[...], gradient, weight_decay, matrix_rate
    )
    for out, value in zip(outs, results):
        out[...] = value


def renew_pieces(place, grads, weight, moment, average):
    seqs, matrices, piece, width = grads.shape
    block = pl.BlockSpec((matrices, piece, width), lambda i, p: (0, i, 0))
    return pl.pallas_call(
        renew_kernel,
        grid_spec=pltpu.PrefetchScalarGridSpec(
            num_scalar_prefetch=1,
            grid=(seqs,),
            in_specs=[pl.BlockSpec(grads.shape, lambda i, p: (0, 0, 0, 0))] + [block] * 3,
            out_specs=[block] * 4,
        ),
        out_shape=[jax.ShapeDtypeStruct(weight.shape, wide)] * 4,
        compiler_params=params(),
        cost_estimate=pl.CostEstimate(
            flops=10 * weight.size, bytes_accessed=30 * weight.size, transcendentals=0
        ),
        name="renew_matrices",
    )(place, grads, weight, moment, average)


def solution(mesh):
    seqs = mesh.shape["seq"]
    hids = mesh.shape["hid"]

    def swap(value, axis, step):
        count = mesh.shape[axis]
        return lax.ppermute(value, axis, [(i, i ^ step) for i in range(count)])

    def gather_pieces(local):
        piece = local.shape[1] // seqs
        own = lax.dynamic_slice_in_dim(local, lax.axis_index("seq") * piece, piece, 1)
        remote = jnp.stack([swap(own, "hid", step) for step in range(1, hids)])
        evens = [remote] + [swap(remote, "seq", other) for other in range(2, seqs, 2)]
        return evens, swap(jnp.stack(evens), "seq", 1)

    def tree_sum(values):
        while len(values) > 1:
            values = [values[i] + values[i + 1] for i in range(0, len(values), 2)]
        return values[0]

    def reduce_pieces(evens, odds):
        added = (evens.astype(wide) + swap(odds, "seq", 1).astype(wide)).astype(low)
        terms = [added[0]] + [swap(added[i], "seq", 2 * i) for i in range(1, seqs // 2)]
        added = tree_sum([term.astype(wide) for term in terms]).astype(low)
        terms = [added[0]] + [swap(added[i], "hid", i) for i in range(1, hids)]
        added = tree_sum([term.astype(wide) for term in terms]).astype(low)
        evens = jnp.stack([added] + [swap(added, "seq", other) for other in range(2, seqs, 2)])
        odds = swap(evens, "seq", 1)
        return jnp.stack([evens, odds], axis=1).reshape((seqs,) + added.shape)

    def reduce_small(value):
        value = tree_sum([value] + [swap(value, "hid", step) for step in range(1, hids)])
        return tree_sum([value] + [swap(value, "seq", step) for step in range(1, seqs)])

    def shards(
        tokens_in,
        image_lengths,
        attn_weight,
        attn_moment,
        attn_average,
        mlp_weight,
        mlp_moment,
        mlp_average,
        vector_params,
        vector_moment,
        vector_average,
        out_grad,
    ):
        packs, rows, width = tokens_in.shape
        share = seqs // packs
        hidden = hids * mlp_weight.shape[1]
        seq_index = lax.axis_index("seq")
        hid_index = lax.axis_index("hid")
        place = jnp.stack([hid_index, seq_index]).astype(jnp.int32)
        attn_piece = attn_weight.shape[0] // seqs
        mlp_piece = mlp_weight.shape[1] // seqs
        aligned = attn_piece % 16 == 0 and mlp_piece % 16 == 0

        def to_packs(array):
            pieces = []
            for other in range(packs):
                piece = lax.dynamic_index_in_dim(
                    array, (seq_index ^ other) % packs, 0, keepdims=False
                )
                pieces.append(swap(piece, "seq", other) if other else piece)
            return jnp.concatenate(pieces, axis=0)

        def to_positions(array):
            own = array[:rows]
            moved = array.astype(low)
            others = [
                swap(moved[other * rows : (other + 1) * rows], "seq", other)
                for other in range(1, packs)
            ]
            return place_packs(place, own, others)

        def across_share(array):
            return [array] + [swap(array, "seq", packs * m) for m in range(1, share)]

        tokens = to_packs(tokens_in)
        order = (seq_index ^ jnp.arange(packs, dtype=jnp.int32)) * rows
        positions = (order[:, None] + jnp.arange(rows, dtype=jnp.int32)[None, :]).reshape(-1)
        lengths = lax.dynamic_index_in_dim(image_lengths, seq_index % packs, 0, keepdims=False)
        ends = jnp.cumsum(lengths)
        query_seg = jnp.sum((ends[None, :] <= positions[:, None]).astype(jnp.int32), axis=1)
        valid = (positions < ends[-1]).astype(wide)[:, None]
        key_seg = jnp.concatenate(across_share(query_seg))

        attn_low = attn_weight.astype(low)
        mlp_low = mlp_weight.astype(low)
        if aligned:
            evens, odds = gather_pieces(attn_low[None])
            whole_attn = assemble(place, attn_low, [e[:, 0] for e in evens], odds[:, :, 0])
        else:
            whole_attn = lax.all_gather(attn_low, "hid", axis=0, tiled=True)
        w_qkv = whole_attn[: 3 * width]
        w_out = whole_attn[3 * width :]

        gain_one, shift_one, bias_query, bias_value, bias_out, gain_two, shift_two, bias_down = [
            vector_params[row_index] for row_index in range(8)
        ]
        hidden_bias = vector_params[8:].reshape(-1)

        tokens_wide = tokens.astype(wide)
        first_norm, first_back = jax.vjp(normalize, tokens_wide, gain_one, shift_one)
        first_low = first_norm.astype(low)
        projected = rows_by_rows(first_low, w_qkv)
        queries = ((projected[:, :width] + bias_query).astype(low) * score_scale).astype(low)
        keys_own = projected[:, width : 2 * width].astype(low)
        values_own = (projected[:, 2 * width :] + bias_value).astype(low)
        keys = jnp.concatenate(across_share(keys_own))
        values = jnp.concatenate(across_share(values_own))
        mixed, log_total = attention_forward(
            queries, keys, values, query_seg[:, None], key_seg[None, :], valid
        )
        residual = tokens_wide + rows_by_rows(mixed, w_out) + bias_out
        second_norm, second_back = jax.vjp(normalize, residual, gain_two, shift_two)
        second_low = second_norm.astype(low)

        grad_low = to_packs(out_grad)
        grad_wide = grad_low.astype(wide)
        if aligned:
            evens, odds = gather_pieces(mlp_low)
            apart = seq_index ^ jnp.arange(seqs)
            away = hid_index ^ jnp.arange(hids)
            bias_pieces = hidden_bias.reshape(hids, seqs, mlp_piece)[away][:, apart]
            mlp_out, second_grad, even_grad, odd_grad, bias_grad = mlp_pieces(
                place,
                second_low,
                grad_low,
                mlp_low,
                evens,
                odds,
                bias_pieces.reshape(hids, 1, seqs * mlp_piece),
            )
            mlp_grad = reduce_pieces(even_grad, odd_grad)
            mlp_new = renew_pieces(place, mlp_grad, mlp_weight, mlp_moment, mlp_average)
            bias_grad = bias_grad.reshape(hids, seqs, mlp_piece)[away][:, apart]
        else:
            whole_mlp = lax.all_gather(mlp_low, "hid", axis=1, tiled=True)
            mlp_out, second_grad, up_grad, down_grad, bias_grad = mlp_plain(
                second_low, grad_low, whole_mlp[0], whole_mlp[1], hidden_bias
            )
            mlp_grad = lax.psum_scatter(
                jnp.stack([up_grad, down_grad]), "hid", scatter_dimension=1, tiled=True
            )
            mlp_grad = lax.psum(mlp_grad, "seq").astype(wide)
            mlp_new = renew(
                mlp_weight, mlp_moment, mlp_average, mlp_grad, weight_decay, matrix_rate
            )
        block_out = to_positions(residual + mlp_out + bias_down)

        residual_part, grad_gain_two, grad_shift_two = second_back(second_grad)
        residual_grad = grad_wide + residual_part
        branch_grad = residual_grad.astype(low)
        mixed_grad = (rows_by_cols(branch_grad, w_out) * valid).astype(low)
        delta = jnp.sum(
            (mixed_grad.astype(wide) * mixed.astype(wide)).reshape(-1, HEADS, HEAD_DIM), axis=2
        )
        delta = jnp.transpose(delta).reshape(HEADS // 2, 2, -1)
        query_grad, key_grad, value_grad = attention_backward(
            queries,
            keys,
            values,
            mixed_grad,
            log_total,
            delta,
            query_seg[None, :],
            key_seg[:, None],
        )
        if share > 1:
            count = queries.shape[0]

            def own_share(array):
                terms = [array[:count].astype(wide)]
                for m in range(1, share):
                    part = array[m * count : (m + 1) * count]
                    terms.append(swap(part, "seq", packs * m).astype(wide))
                return tree_sum(terms).astype(low)

            key_grad = own_share(key_grad)
            value_grad = own_share(value_grad)
        if aligned:
            attn_grad = matrix_grads(
                place,
                seqs,
                hids,
                query_grad,
                key_grad,
                value_grad,
                branch_grad,
                first_low,
                mixed,
            )[:, :, None]
            attn_grad = reduce_pieces(attn_grad[: seqs // 2], attn_grad[seqs // 2 :])
            attn_new = renew_pieces(
                place, attn_grad, attn_weight[None], attn_moment[None], attn_average[None]
            )
            attn_new = [array[0] for array in attn_new]
        else:
            attn_grad = [
                cols_by_cols(query_grad, first_low),
                cols_by_cols(key_grad, first_low),
                cols_by_cols(value_grad, first_low),
                cols_by_cols(branch_grad, mixed),
            ]
            attn_grad = lax.psum_scatter(
                jnp.concatenate(attn_grad).astype(low), "hid", scatter_dimension=0, tiled=True
            )
            attn_grad = lax.psum(attn_grad, "seq").astype(wide)
            attn_new = renew(
                attn_weight, attn_moment, attn_average, attn_grad, weight_decay, matrix_rate
            )
        joined_grad = jnp.concatenate([query_grad, key_grad, value_grad], axis=1)
        first_grad = rows_by_cols(joined_grad, w_qkv)
        input_part, grad_gain_one, grad_shift_one = first_back(first_grad)
        input_grad = to_positions(residual_grad + input_part)

        vector_grad = jnp.concatenate(
            [
                jnp.stack(
                    [
                        grad_gain_one,
                        grad_shift_one,
                        jnp.sum(query_grad.astype(wide), axis=0),
                        jnp.sum(value_grad.astype(wide), axis=0),
                        jnp.sum(branch_grad.astype(wide), axis=0),
                        grad_gain_two,
                        grad_shift_two,
                        jnp.sum(grad_wide, axis=0),
                    ]
                ),
                bias_grad.reshape(-1, width),
            ]
        )
        vector_grad = reduce_small(vector_grad)
        vector_new = renew(
            vector_params, vector_moment, vector_average, vector_grad, 0.0, vector_rate
        )
        return (block_out, input_grad, *attn_new, *mlp_new, *vector_new)

    return jax.shard_map(
        shards,
        mesh=mesh,
        in_specs=(
            P("hid", "seq", None),
            P("hid", None),
            P("hid", None),
            P("hid", None),
            P("hid", None),
            P(None, "hid", None),
            P(None, "hid", None),
            P(None, "hid", None),
            P(),
            P(),
            P(),
            P("hid", "seq", None),
        ),
        out_specs=(
            P("hid", "seq", None),
            P("hid", "seq", None),
            P("hid", None),
            P("hid", None),
            P("hid", None),
            P("hid", None),
            P(None, "hid", None),
            P(None, "hid", None),
            P(None, "hid", None),
            P(None, "hid", None),
            P(),
            P(),
            P(),
            P(),
        ),
        check_vma=False,
    )
```

time: 1240 us -> 531 us (0.43)
  waiting for transfers between devices: 737 us -> 182 us
  matrix products: 267 us -> 20.2 us
  Pallas kernels: 0 us -> 150 us
  starting transfers between devices: 0.75 us -> 89.4 us
  local copies, waits for them, and re-layouts: 86.9 us -> 34.9 us
  blocking collectives: 41.9 us -> 0 us
  other arithmetic: 81 us -> 46.3 us
  between operations: 14.9 us -> 1.87 us
    all_gather x5 -> x0, waiting for transfers between devices: 347 us -> none  [the longest x1 108 us: shards(): group_inputs = lax.all_gather(second_low, 'hid', axis=0, tiled=True)]
    reduce_scatter x5 -> x0, waiting for transfers between devices: 317 us -> none  [the longest x1 111 us: shards(): lax.psum_scatter(piece_grads.astype(jnp.bfloat16), 'hid', scatter_dimensi...]
    dot_general x18 -> x4, matrix products: 267 us -> 20.2 us  [the longest x2 11 us: rows_by_cols(): lax.dot_general(a, b, (((1,), (0,)), ((), ())), preferred_element_type=wide)]
    ppermute x0 -> x74, waiting for transfers between devices: none -> 182 us  [swap(): return lax.ppermute(value, axis, [(i, i ^ step) for i in range(count)])]
    pallas_call x0 -> x9, Pallas kernels: none -> 150 us  [the longest x1 41.7 us: mlp_pieces(): pl.pallas_call(functools.partial(mlp_pieces_kernel, halves), grid_spec=pl...]
    ppermute x0 -> x74, starting transfers between devices: none -> 89.4 us  [swap(): return lax.ppermute(value, axis, [(i, i ^ step) for i in range(count)])]
    psum x1 -> x0, waiting for transfers between devices: 71.7 us -> none  [shards(): lax.psum(attn_part, 'seq').astype(jnp.float32)]
    psum x2 -> x0, blocking collectives: 41.9 us -> none  [the longest x1 25.9 us: shards(): lax.psum(vector_part.astype(jnp.bfloat16), 'seq').astype(jnp.float32)]
  transfers between devices with their start and end apart: 11 -> 74, of which waited for: 10 -> 25; matrix products, arithmetic and copies ran while one was open for 21% -> 14% of each run, Pallas kernels for 0% -> 18%
where the time goes in v1:
time: 531 us; the launch traced here: 525 us
  waiting for transfers between devices  182 us (34%)
  Pallas kernels  150 us (28%)
  starting transfers between devices  89.4 us (17%)
  other arithmetic  46.3 us (9%)
  local copies, waits for them, and re-layouts  34.9 us (7%)
  matrix products  20.2 us (4%)
    ppermute x74, waiting for transfers between devices, swap(): return lax.ppermute(value, axis, [(i, i ^ step) for i in range(count)])  182 us
    ppermute x74, starting transfers between devices, swap(): return lax.ppermute(value, axis, [(i, i ^ step) for i in range(count)])  89.4 us
    pallas_call x1, Pallas kernels, mlp_pieces(): pl.pallas_call(functools.partial(mlp_pieces_kernel, halves), grid_spec=pl...  41.7 us
    pallas_call x1, Pallas kernels, attention_backward(): pl.pallas_call(functools.partial(attention_backward_kernel, min(256, rows...  39.6 us
    pallas_call x2, Pallas kernels, renew_pieces(): pl.pallas_call(renew_kernel, grid_spec=pltpu.PrefetchScalarGridSpec(num_s...  25.3 us
    pallas_call x1, Pallas kernels, attention_forward(): pl.pallas_call(functools.partial(attention_forward_kernel, min(128, rows)...  21 us
    pallas_call x1, Pallas kernels, matrix_grads(): pl.pallas_call(functools.partial(matrix_grads_kernel, seqs), in_specs=[sm...  11 us
    dot_general x2, matrix products, rows_by_cols(): lax.dot_general(a, b, (((1,), (0,)), ((), ())), preferred_element_type=wide)  11 us
  transfers between devices with their start and end apart: 74, of which 25 were waited for; matrix products, arithmetic and copies ran while one was open for 14% of the time, Pallas kernels for 18%

profile of v1, /device:TPU:9, one launch (start us, length us, event | category | flops | bytes accessed | tf_op | source)
XLA Modules:
  0.0 524.6 jit_solution(12500325652841743429)
XLA Ops:
  3.4 2.5 collective-permute-start.8
  10.7 2.5 dynamic-slice_bitcast_fusion
  16.2 2.6 convert_element_type.189.local_ref
  36.1 9.9 %collective-permute-done.4 = bf16[128,768]{1,0:T(8,128)(2,1)S(1)} collective-permute-done((bf16[128,768]{1,0:T(8,128)(2,1)}, bf16[128,768]{1,0:T(8,128)(2,1)S(1)}, u32[]{:S(2)}, u32[]{:S(2)}) %collective-permute-start.4) | collective-permute-done | bytes 196640 | tf_op jit(solution)/shard_map/ppermute | solution.py:492
  54.3 2.5 collective-permute-start.22
  57.0 4.3 collective-permute-done.10
  62.6 11.7 %collective-permute-start.18 = (bf16[128,768]{1,0:T(8,128)(2,1)S(1)}, bf16[128,768]{1,0:T(8,128)(2,1)S(1)}, u32[]{:S(2)}, u32[]{:S(2)}) collective-permute-start(bf16[128,768]{1,0:T(8,128)(2,1)S(1)} %copy-done.42), channel_id=1, source_target_pairs={{0,20},{4,16},{8,28},{12,24},{16,4},{20,0},{24,12},{28,8},{1,21},{... | collective-permute-start | bytes 589832 | tf_op jit(solution)/shard_map/ppermute | solution.py:492
  74.6 5.4 %collective-permute-done.18 = bf16[128,768]{1,0:T(8,128)(2,1)S(1)} collective-permute-done((bf16[128,768]{1,0:T(8,128)(2,1)S(1)}, bf16[128,768]{1,0:T(8,128)(2,1)S(1)}, u32[]{:S(2)}, u32[]{:S(2)}) %collective-permute-start.18) | collective-permute-done | bytes 196640 | tf_op jit(solution)/shard_map/ppermute | solution.py:492
  80.0 2.9 collective-permute-start.20
  87.4 5.1 collective-permute-done.20
  95.0 12.5 %collective-permute-done.24.refs_1_ = bf16[3,2,96,768]{3,2,1,0:T(8,128)(2,1)S(1)} collective-permute-done((bf16[3,2,96,768]{3,2,1,0:T(8,128)(2,1)S(1)}, bf16[3,2,96,768]{3,2,1,0:T(8,128)(2,1)S(1)}, u32[]{:S(2)}, u32[]{:S(2)}) %collective-permute-start.24) | collective-permute-done | bytes 884768 | tf_op jit(solution)/shard_map/ppermute | solution.py:492
  107.5 4.0 collective-permute-done.25.refs_2_
  111.5 17.8 %collective-permute-done.26.refs_3_ = bf16[3,2,96,768]{3,2,1,0:T(8,128)(2,1)S(1)} collective-permute-done((bf16[3,2,96,768]{3,2,1,0:T(8,128)(2,1)S(1)}, bf16[3,2,96,768]{3,2,1,0:T(8,128)(2,1)S(1)}, u32[]{:S(2)}, u32[]{:S(2)}) %collective-permute-start.26) | collective-permute-done | bytes 884768 | tf_op jit(solution)/shard_map/ppermute | solution.py:492
  129.3 2.5 pad_maximum_fusion
  134.2 5.0 assemble_rows.1
  139.1 5.9 %fusion.22 = f32[1024,2304]{1,0:T(8,128)S(1)} fusion(bf16[1024,768]{1,0:T(8,128)(2,1)S(1)} %copy-done.18, bf16[3072,768]{1,0:T(8,128)(2,1)} %assemble_rows.1), kind=kOutput, calls=%fused_computation.50 | convolution fusion | flops 3623878656 | bytes 14548992 | tf_op jit(solution)/shard_map/dot_general | solution.py:28
  148.5 21.0 %attention_forward.1 = (bf16[1024,768]{1,0:T(8,128)(2,1)}, f32[6,2,1024]{2,1,0:T(2,128)}) custom-call(bf16[1024,768]{1,0:T(8,128)(2,1)} %get-tuple-element.78.q_ref, bf16[1024,768]{1,0:T(8,128)(2,1)} %get-tuple-element.77.k_ref, bf16[1024,768]{1,0:T(8,128)(2,1)} %fusion.19.v_ref, s32[1024,1]{1,0:T(8,128)} %copy.93.query_seg.key_seg, s32[1,1024]{1,0:T(1,128)} %bitcast.209, ...), custom_call_target="tpu_custom_call" | custom-call | flops 16106127360 | bytes 6291456 | tf_op jit(solution)/shard_map/attention_forward/pallas_call | solution.py:98
  169.5 3.3 fusion.59
  175.1 41.7 %mlp_both_ways.1 = (f32[1024,768]{1,0:T(8,128)}, f32[1024,768]{1,0:T(8,128)}, bf16[4,4,2,96,768]{4,3,2,1,0:T(8,128)(2,1)}, bf16[4,4,2,96,768]{4,3,2,1,0:T(8,128)(2,1)}, f32[4,1,768]{2,1,0:T(1,128)}) custom-call(s32[2]{0:T(128)} %pad_add_fusion.place, bf16[1024,768]{1,0:T(8,128)(2,1)} %add_convert_fusion.1.a_ref, bf16[1024,768]{1,0:T(8,128)(2,1)} %copy-done.5, ...), custom_call_target="tpu_custom_call" | custom-call | flops 28991029248 | bytes 18874368 | tf_op jit(solution)/shard_map/mlp_both_ways/pallas_call | solution.py:342
  216.8 3.1 multiply_reduce_fusion
  220.6 3.1 fusion.54
  226.2 4.9 convert_multiply_fusion
  231.1 3.5 copy.99
  237.6 39.6 %attention_backward.1 = (bf16[1024,768]{1,0:T(8,128)(2,1)}, bf16[1024,768]{1,0:T(8,128)(2,1)}, bf16[1024,768]{1,0:T(8,128)(2,1)}) custom-call(bf16[1024,768]{1,0:T(8,128)(2,1)} %get-tuple-element.78.q_ref, bf16[1024,768]{1,0:T(8,128)(2,1)} %get-tuple-element.77.k_ref, bf16[1024,768]{1,0:T(8,128)(2,1)} %fusion.19.v_ref, ...), custom_call_target="tpu_custom_call" | custom-call | flops 32212254720 | bytes 11010048 | tf_op jit(solution)/shard_map/attention_backward/pallas_call | solution.py:182
  277.1 11.0 %matrix_grads.1 = bf16[8,4,96,768]{3,2,1,0:T(8,128)(2,1)} custom-call(s32[2]{0:T(128)} %pad_add_fusion.place, bf16[1024,768]{1,0:T(8,128)(2,1)} %get-tuple-element.36.dq, bf16[1024,768]{1,0:T(8,128)(2,1)} %get-tuple-element.37.dk, bf16[1024,768]{1,0:T(8,128)(2,1)} %get-tuple-element.38.dv, bf16[1024,768]{1,0:T(8,128)(2,1)} %copy-done.7, ...), custom_call_target="tpu_custom_call" | custom-call | flops 4831838208 | bytes 9437184 | tf_op jit(solution)/shard_map/matrix_grads/pallas_call | solution.py:441
  288.2 3.4 slice_bitcast_fusion
  292.0 6.1 %fusion.51 = (f32[768]{0:T(1024)S(1)}, f32[1024]{0:T(1024)S(1)}, f32[1024,768]{1,0:T(8,128)S(1)}) fusion(f32[768]{0:T(1024)S(1)} %get-tuple-element.64, f32[1024]{0:T(1024)S(1)} %broadcast_multiply_fusion.1, bf16[1024,768]{1,0:T(8,128)(2,1)S(1)} %constant_dynamic-update-slice_fusion, bf16[3072,768]{1,0:T(8,128)(2,1)} %assemble_rows.1, ...), kind=kOutput, calls=%fused_computation.172 | convolution fusion | flops 3642751232 | bytes 12990464 | tf_op jit(solution)/shard_map/dot_general | solution.py:32
  300.0 3.2 fusion.53
  308.9 5.6 %add_convert_fusion = bf16[4,4,2,96,768]{4,3,2,1,0:T(8,128)(2,1)S(1)} fusion(bf16[4,4,2,96,768]{4,3,2,1,0:T(8,128)(2,1)} %collective-permute-done.53, bf16[4,4,2,96,768]{4,3,2,1,0:T(8,128)(2,1)} %get-tuple-element.43), kind=kLoop, calls=%fused_computation.4 | loop fusion | flops 9437184 | bytes 14155776 | tf_op jit(solution)/shard_map/convert_element_type | solution.py:507
  315.2 2.4 collective-permute-start.56
  319.1 2.4 fusion.10
  321.6 20.2 %collective-permute-done.54 = bf16[4,2,96,768]{3,2,1,0:T(8,128)(2,1)S(1)} collective-permute-done((bf16[4,2,96,768]{3,2,1,0:T(8,128)(2,1)S(1)}, bf16[4,2,96,768]{3,2,1,0:T(8,128)(2,1)S(1)}, u32[]{:S(2)}, u32[]{:S(2)}) %collective-permute-start.54) | collective-permute-done | bytes 1179680 | tf_op jit(solution)/shard_map/ppermute | solution.py:492
  342.8 23.4 %collective-permute-done.56 = bf16[4,2,96,768]{3,2,1,0:T(8,128)(2,1)S(1)} collective-permute-done((bf16[4,2,96,768]{3,2,1,0:T(8,128)(2,1)S(1)}, bf16[4,2,96,768]{3,2,1,0:T(8,128)(2,1)S(1)}, u32[]{:S(2)}, u32[]{:S(2)}) %collective-permute-start.56) | collective-permute-done | bytes 1179680 | tf_op jit(solution)/shard_map/ppermute | solution.py:492
  369.1 11.7 %collective-permute-done.43 = bf16[4,1,96,768]{3,2,0,1:T(8,128)(2,1)S(1)} collective-permute-done((bf16[4,1,96,768]{3,2,0,1:T(8,128)(2,1)S(1)}, bf16[4,1,96,768]{3,2,0,1:T(8,128)(2,1)S(1)}, u32[]{:S(2)}, u32[]{:S(2)}) %collective-permute-start.43) | collective-permute-done | bytes 589856 | tf_op jit(solution)/shard_map/ppermute | solution.py:492
  383.8 8.8 %collective-permute-done.45 = bf16[4,1,96,768]{3,2,0,1:T(8,128)(2,1)S(1)} collective-permute-done((bf16[4,1,96,768]{3,2,0,1:T(8,128)(2,1)S(1)}, bf16[4,1,96,768]{3,2,0,1:T(8,128)(2,1)S(1)}, u32[]{:S(2)}, u32[]{:S(2)}) %collective-permute-start.45) | collective-permute-done | bytes 589856 | tf_op jit(solution)/shard_map/ppermute | solution.py:492
  394.2 4.9 collective-permute-start.69
  399.1 11.2 %collective-permute-done.59 = bf16[2,96,768]{2,1,0:T(8,128)(2,1)S(1)} collective-permute-done((bf16[2,96,768]{2,1,0:T(8,128)(2,1)S(1)}, bf16[2,96,768]{2,1,0:T(8,128)(2,1)S(1)}, u32[]{:S(2)}, u32[]{:S(2)}) %collective-permute-start.59) | collective-permute-done | bytes 294944 | tf_op jit(solution)/shard_map/ppermute | solution.py:492
  410.6 6.9 %collective-permute-start.71 = (f32[12,768]{1,0:T(8,128)S(1)}, f32[12,768]{1,0:T(8,128)S(1)}, u32[]{:S(2)}, u32[]{:S(2)}) collective-permute-start(f32[12,768]{1,0:T(8,128)S(1)} %add_add_fusion.5), channel_id=1, source_target_pairs={{0,20},{4,16},{8,28},{12,24},{16,4},{20,0},{24,12},{28,8},{1,21},{... | collective-permute-start | bytes 110600 | tf_op jit(solution)/shard_map/ppermute | solution.py:492
  421.3 11.1 %collective-permute-done.61 = bf16[2,96,768]{2,1,0:T(8,128)(2,1)S(1)} collective-permute-done((bf16[2,96,768]{2,1,0:T(8,128)(2,1)S(1)}, bf16[2,96,768]{2,1,0:T(8,128)(2,1)S(1)}, u32[]{:S(2)}, u32[]{:S(2)}) %collective-permute-start.61) | collective-permute-done | bytes 294944 | tf_op jit(solution)/shard_map/ppermute | solution.py:492
  445.7 4.3 collective-permute-done.37.refs_2_
  450.4 2.5 collective-permute-start.51
  453.1 9.8 %collective-permute-done.50 = bf16[1,96,768]{2,1,0:T(8,128)(2,1)S(1)} collective-permute-done((bf16[1,96,768]{2,1,0:T(8,128)(2,1)S(1)}, bf16[1,96,768]{2,1,0:T(8,128)(2,1)S(1)}, u32[]{:S(2)}, u32[]{:S(2)}) %collective-permute-start.50) | collective-permute-done | bytes 147488 | tf_op jit(solution)/shard_map/ppermute | solution.py:492
  465.9 5.4 %collective-permute-done.41.refs_6_ = bf16[128,768]{1,0:T(8,128)(2,1)S(1)} collective-permute-done((bf16[128,768]{1,0:T(8,128)(2,1)S(1)}, bf16[128,768]{1,0:T(8,128)(2,1)S(1)}, u32[]{:S(2)}, u32[]{:S(2)}) %collective-permute-start.41) | collective-permute-done | bytes 196640 | tf_op jit(solution)/shard_map/ppermute | solution.py:492
  482.5 3.4 place_packs.3
  485.9 5.4 %collective-permute-done.32.refs_4_ = bf16[128,768]{1,0:T(8,128)(2,1)S(1)} collective-permute-done((bf16[128,768]{1,0:T(8,128)(2,1)S(1)}, bf16[128,768]{1,0:T(8,128)(2,1)S(1)}, u32[]{:S(2)}, u32[]{:S(2)}) %collective-permute-start.32) | collective-permute-done | bytes 196640 | tf_op jit(solution)/shard_map/ppermute | solution.py:492
  492.7 3.4 place_packs.2
  497.3 9.9 %renew_matrices.2 = (f32[1,768,768]{2,1,0:T(8,128)}, f32[1,768,768]{2,1,0:T(8,128)}, f32[1,768,768]{2,1,0:T(8,128)}, f32[1,768,768]{2,1,0:T(8,128)}) custom-call(s32[2]{0:T(128)} %pad_add_fusion.place, bf16[8,1,96,768]{3,2,1,0:T(8,128)(2,1)} %bitcast.176, f32[1,768,768]{2,1,0:T(8,128)} %bitcast.173, f32[1,768,768]{2,1,0:T(8,128)} %bitcast.177, ...), custom_call_target="tpu_custom_call" | custom-call | flops 5898240 | bytes 17694720 | tf_op jit(solution)/shard_map/renew_matrices/pallas_call | solution.py:469
  509.1 15.3 %renew_matrices.3 = (f32[2,768,768]{2,1,0:T(8,128)}, f32[2,768,768]{2,1,0:T(8,128)}, f32[2,768,768]{2,1,0:T(8,128)}, f32[2,768,768]{2,1,0:T(8,128)}) custom-call(s32[2]{0:T(128)} %pad_add_fusion.place, bf16[8,2,96,768]{3,2,1,0:T(8,128)(2,1)} %bitcast.170, f32[2,768,768]{2,1,0:T(8,128)} %weight.1, f32[2,768,768]{2,1,0:T(8,128)} %moment.1, f32[2,768,768]{2,1,0:T(8,128)} %average.1), custom_call_target="tpu_custom_call" | custom-call | flops 11796480 | bytes 35389440 | tf_op jit(solution)/shard_map/renew_matrices/pallas_call | solution.py:469
  (343 shorter events, 113.8 us)
Async XLA Ops:
  3.4 22.4 %collective-permute-start.7 = (bf16[1,96,768]{2,1,0:T(8,128)(2,1)}, bf16[1,96,768]{2,1,0:T(8,128)(2,1)}, u32[]{:S(2)}, u32[]{:S(2)}) collective-permute-start(bf16[1,96,768]{2,1,0:T(8,128)(2,1)} %dynamic-slice_bitcast_fusion.14), channel_id=1, source_target_pairs={{0,1},{1,0},{2,3},{3,2},{4,5},{5,4},{6,7},{7,6},{8,9},{9,8},{10,11... | collective-permute-start | bytes 442376 | tf_op jit(solution)/shard_map/ppermute | solution.py:492
  3.4 22.8 %collective-permute-start.8 = (bf16[1,96,768]{2,1,0:T(8,128)(2,1)}, bf16[1,96,768]{2,1,0:T(8,128)(2,1)}, u32[]{:S(2)}, u32[]{:S(2)}) collective-permute-start(bf16[1,96,768]{2,1,0:T(8,128)(2,1)} %dynamic-slice_bitcast_fusion.14), channel_id=1, source_target_pairs={{0,2},{1,3},{2,0},{3,1},{4,6},{5,7},{6,4},{7,5},{8,10},{9,11},{10,... | collective-permute-start | bytes 442376 | tf_op jit(solution)/shard_map/ppermute | solution.py:492
  5.8 21.6 %collective-permute-start.9 = (bf16[1,96,768]{2,1,0:T(8,128)(2,1)}, bf16[1,96,768]{2,1,0:T(8,128)(2,1)}, u32[]{:S(2)}, u32[]{:S(2)}) collective-permute-start(bf16[1,96,768]{2,1,0:T(8,128)(2,1)} %dynamic-slice_bitcast_fusion.14), channel_id=1, source_target_pairs={{0,3},{1,2},{2,1},{3,0},{4,7},{5,6},{6,5},{7,4},{8,11},{9,10},{10,... | collective-permute-start | bytes 442376 | tf_op jit(solution)/shard_map/ppermute | solution.py:492
  7.1 22.8 %collective-permute-start = (bf16[128,768]{1,0:T(8,128)(2,1)}, bf16[128,768]{1,0:T(8,128)(2,1)}, u32[]{:S(2)}, u32[]{:S(2)}) collective-permute-start(bf16[128,768]{1,0:T(8,128)(2,1)} %get-tuple-element.113), channel_id=1, source_target_pairs={{0,4},{4,0},{8,12},{12,8},{16,20},{20,16},{24,28},{28,24},{1,5},{5... | collective-permute-start | bytes 589832 | tf_op jit(solution)/shard_map/ppermute | solution.py:492
  8.6 24.4 %collective-permute-start.1 = (bf16[128,768]{1,0:T(8,128)(2,1)}, bf16[128,768]{1,0:T(8,128)(2,1)}, u32[]{:S(2)}, u32[]{:S(2)}) collective-permute-start(bf16[128,768]{1,0:T(8,128)(2,1)} %get-tuple-element.112), channel_id=1, source_target_pairs={{0,8},{4,12},{8,0},{12,4},{16,24},{20,28},{24,16},{28,20},{1,9},{5... | collective-permute-start | bytes 589832 | tf_op jit(solution)/shard_map/ppermute | solution.py:492
  27.4 18.5 %collective-permute-start.4 = (bf16[128,768]{1,0:T(8,128)(2,1)}, bf16[128,768]{1,0:T(8,128)(2,1)S(1)}, u32[]{:S(2)}, u32[]{:S(2)}) collective-permute-start(bf16[128,768]{1,0:T(8,128)(2,1)} %get-tuple-element.109), channel_id=1, source_target_pairs={{0,20},{4,16},{8,28},{12,24},{16,4},{20,0},{24,12},{28,8},{1,21},{... | collective-permute-start | bytes 589832 | tf_op jit(solution)/shard_map/ppermute | solution.py:492
  29.9 16.9 %collective-permute-start.5 = (bf16[128,768]{1,0:T(8,128)(2,1)}, bf16[128,768]{1,0:T(8,128)(2,1)S(1)}, u32[]{:S(2)}, u32[]{:S(2)}) collective-permute-start(bf16[128,768]{1,0:T(8,128)(2,1)} %get-tuple-element.114), channel_id=1, source_target_pairs={{0,24},{4,28},{8,16},{12,20},{16,8},{20,12},{24,0},{28,4},{1,25},{... | collective-permute-start | bytes 589832 | tf_op jit(solution)/shard_map/ppermute | solution.py:492
  33.1 15.1 %collective-permute-start.6 = (bf16[128,768]{1,0:T(8,128)(2,1)}, bf16[128,768]{1,0:T(8,128)(2,1)S(1)}, u32[]{:S(2)}, u32[]{:S(2)}) collective-permute-start(bf16[128,768]{1,0:T(8,128)(2,1)} %get-tuple-element.108), channel_id=1, source_target_pairs={{0,28},{4,24},{8,20},{12,16},{16,12},{20,8},{24,4},{28,0},{1,29},{... | collective-permute-start | bytes 589832 | tf_op jit(solution)/shard_map/ppermute | solution.py:492
  34.5 14.2 %collective-permute-start.14 = (bf16[128,768]{1,0:T(8,128)(2,1)S(1)}, bf16[128,768]{1,0:T(8,128)(2,1)S(1)}, u32[]{:S(2)}, u32[]{:S(2)}) collective-permute-start(bf16[128,768]{1,0:T(8,128)(2,1)S(1)} %copy-done.46), channel_id=1, source_target_pairs={{0,4},{4,0},{8,12},{12,8},{16,20},{20,16},{24,28},{28,24},{1,5},{5... | collective-permute-start | bytes 589832 | tf_op jit(solution)/shard_map/ppermute | solution.py:492
  34.8 14.2 %collective-permute-start.15 = (bf16[128,768]{1,0:T(8,128)(2,1)S(1)}, bf16[128,768]{1,0:T(8,128)(2,1)S(1)}, u32[]{:S(2)}, u32[]{:S(2)}) collective-permute-start(bf16[128,768]{1,0:T(8,128)(2,1)S(1)} %copy-done.45), channel_id=1, source_target_pairs={{0,8},{4,12},{8,0},{12,4},{16,24},{20,28},{24,16},{28,20},{1,9},{5... | collective-permute-start | bytes 589832 | tf_op jit(solution)/shard_map/ppermute | solution.py:492
  48.2 13.1 %collective-permute-start.10 = (bf16[3,1,96,768]{3,2,0,1:T(8,128)(2,1)S(1)}, bf16[3,1,96,768]{3,2,0,1:T(8,128)(2,1)S(1)}, u32[]{:S(2)}, u32[]{:S(2)}) collective-permute-start(bf16[3,1,96,768]{3,2,0,1:T(8,128)(2,1)S(1)} %get-tuple-element.128), channel_id=1, source_target_pairs={{0,8},{4,12},{8,0},{12,4},{16,24},{20,28},{24,16},{28,20},{1,9},{5... | collective-permute-start | bytes 1327112 | tf_op jit(solution)/shard_map/ppermute | solution.py:492
  48.6 14.0 %collective-permute-start.11 = (bf16[3,1,96,768]{3,2,0,1:T(8,128)(2,1)S(1)}, bf16[3,1,96,768]{3,2,0,1:T(8,128)(2,1)S(1)}, u32[]{:S(2)}, u32[]{:S(2)}) collective-permute-start(bf16[3,1,96,768]{3,2,0,1:T(8,128)(2,1)S(1)} %get-tuple-element.128), channel_id=1, source_target_pairs={{0,16},{4,20},{8,24},{12,28},{16,0},{20,4},{24,8},{28,12},{1,17},{... | collective-permute-start | bytes 1327112 | tf_op jit(solution)/shard_map/ppermute | solution.py:492
  49.0 25.4 %collective-permute-start.12 = (bf16[3,1,96,768]{3,2,0,1:T(8,128)(2,1)S(1)}, bf16[3,1,96,768]{3,2,0,1:T(8,128)(2,1)S(1)}, u32[]{:S(2)}, u32[]{:S(2)}) collective-permute-start(bf16[3,1,96,768]{3,2,0,1:T(8,128)(2,1)S(1)} %get-tuple-element.128), channel_id=1, source_target_pairs={{0,24},{4,28},{8,16},{12,20},{16,8},{20,12},{24,0},{28,4},{1,25},{... | collective-permute-start | bytes 1327112 | tf_op jit(solution)/shard_map/ppermute | solution.py:492
  53.4 26.6 %collective-permute-start.21 = (bf16[2,96,768]{2,1,0:T(8,128)(2,1)S(1)}, bf16[2,96,768]{2,1,0:T(8,128)(2,1)S(1)}, u32[]{:S(2)}, u32[]{:S(2)}) collective-permute-start(bf16[2,96,768]{2,1,0:T(8,128)(2,1)S(1)} %constant_dynamic-slice_fusion), channel_id=1, source_target_pairs={{0,1},{1,0},{2,3},{3,2},{4,5},{5,4},{6,7},{7,6},{8,9},{9,8},{10,11... | collective-permute-start | bytes 884744 | tf_op jit(solution)/shard_map/ppermute | solution.py:492
  54.3 28.7 %collective-permute-start.22 = (bf16[2,96,768]{2,1,0:T(8,128)(2,1)S(1)}, bf16[2,96,768]{2,1,0:T(8,128)(2,1)S(1)}, u32[]{:S(2)}, u32[]{:S(2)}) collective-permute-start(bf16[2,96,768]{2,1,0:T(8,128)(2,1)S(1)} %constant_dynamic-slice_fusion), channel_id=1, source_target_pairs={{0,2},{1,3},{2,0},{3,1},{4,6},{5,7},{6,4},{7,5},{8,10},{9,11},{10,... | collective-permute-start | bytes 884744 | tf_op jit(solution)/shard_map/ppermute | solution.py:492
  61.3 21.7 %collective-permute-start.23 = (bf16[2,96,768]{2,1,0:T(8,128)(2,1)S(1)}, bf16[2,96,768]{2,1,0:T(8,128)(2,1)S(1)}, u32[]{:S(2)}, u32[]{:S(2)}) collective-permute-start(bf16[2,96,768]{2,1,0:T(8,128)(2,1)S(1)} %constant_dynamic-slice_fusion), channel_id=1, source_target_pairs={{0,3},{1,2},{2,1},{3,0},{4,7},{5,6},{6,5},{7,4},{8,11},{9,10},{10,... | collective-permute-start | bytes 884744 | tf_op jit(solution)/shard_map/ppermute | solution.py:492
  62.6 17.4 %collective-permute-start.18 = (bf16[128,768]{1,0:T(8,128)(2,1)S(1)}, bf16[128,768]{1,0:T(8,128)(2,1)S(1)}, u32[]{:S(2)}, u32[]{:S(2)}) collective-permute-start(bf16[128,768]{1,0:T(8,128)(2,1)S(1)} %copy-done.42), channel_id=1, source_target_pairs={{0,20},{4,16},{8,28},{12,24},{16,4},{20,0},{24,12},{28,8},{1,21},{... | collective-permute-start | bytes 589832 | tf_op jit(solution)/shard_map/ppermute | solution.py:492
  74.5 58.4 %collective-permute-start.13 = (bf16[4,3,1,96,768]{4,3,1,0,2:T(8,128)(2,1)S(1)}, bf16[4,3,1,96,768]{4,3,1,0,2:T(8,128)(2,1)S(1)}, u32[]{:S(2)}, u32[]{:S(2)}) collective-permute-start(bf16[4,3,1,96,768]{4,3,1,0,2:T(8,128)(2,1)S(1)} %pad_maximum_fusion.2), channel_id=1, source_target_pairs={{0,4},{4,0},{8,12},{12,8},{16,20},{20,16},{24,28},{28,24},{1,5},{5... | collective-permute-start | bytes 5308424 | tf_op jit(solution)/shard_map/ppermute | solution.py:492
  80.0 12.5 %collective-permute-start.20 = (bf16[128,768]{1,0:T(8,128)(2,1)S(1)}, bf16[128,768]{1,0:T(8,128)(2,1)S(1)}, u32[]{:S(2)}, u32[]{:S(2)}) collective-permute-start(bf16[128,768]{1,0:T(8,128)(2,1)S(1)} %copy-done.40), channel_id=1, source_target_pairs={{0,28},{4,24},{8,20},{12,16},{16,12},{20,8},{24,4},{28,0},{1,29},{... | collective-permute-start | bytes 589832 | tf_op jit(solution)/shard_map/ppermute | solution.py:492
  83.1 24.4 %collective-permute-start.24 = (bf16[3,2,96,768]{3,2,1,0:T(8,128)(2,1)S(1)}, bf16[3,2,96,768]{3,2,1,0:T(8,128)(2,1)S(1)}, u32[]{:S(2)}, u32[]{:S(2)}) collective-permute-start(bf16[3,2,96,768]{3,2,1,0:T(8,128)(2,1)S(1)} %get-tuple-element.121.refs_0_), channel_id=1, source_target_pairs={{0,8},{4,12},{8,0},{12,4},{16,24},{20,28},{24,16},{28,20},{1,9},{5... | collective-permute-start | bytes 2654216 | tf_op jit(solution)/shard_map/ppermute | solution.py:492
  85.0 26.5 %collective-permute-start.25 = (bf16[3,2,96,768]{3,2,1,0:T(8,128)(2,1)S(1)}, bf16[3,2,96,768]{3,2,1,0:T(8,128)(2,1)S(1)}, u32[]{:S(2)}, u32[]{:S(2)}) collective-permute-start(bf16[3,2,96,768]{3,2,1,0:T(8,128)(2,1)S(1)} %get-tuple-element.121.refs_0_), channel_id=1, source_target_pairs={{0,16},{4,20},{8,24},{12,28},{16,0},{20,4},{24,8},{28,12},{1,17},{... | collective-permute-start | bytes 2654216 | tf_op jit(solution)/shard_map/ppermute | solution.py:492
  87.1 42.2 %collective-permute-start.26 = (bf16[3,2,96,768]{3,2,1,0:T(8,128)(2,1)S(1)}, bf16[3,2,96,768]{3,2,1,0:T(8,128)(2,1)S(1)}, u32[]{:S(2)}, u32[]{:S(2)}) collective-permute-start(bf16[3,2,96,768]{3,2,1,0:T(8,128)(2,1)S(1)} %get-tuple-element.121.refs_0_), channel_id=1, source_target_pairs={{0,24},{4,28},{8,16},{12,20},{16,8},{20,12},{24,0},{28,4},{1,25},{... | collective-permute-start | bytes 2654216 | tf_op jit(solution)/shard_map/ppermute | solution.py:492
  131.7 43.3 %collective-permute-start.27 = (bf16[4,3,2,96,768]{4,3,2,1,0:T(8,128)(2,1)}, bf16[4,3,2,96,768]{4,3,2,1,0:T(8,128)(2,1)}, u32[]{:S(2)}, u32[]{:S(2)}) collective-permute-start(bf16[4,3,2,96,768]{4,3,2,1,0:T(8,128)(2,1)} %pad_maximum_fusion), channel_id=1, source_target_pairs={{0,4},{4,0},{8,12},{12,8},{16,20},{20,16},{24,28},{28,24},{1,5},{5... | collective-permute-start | bytes 10616840 | tf_op jit(solution)/shard_map/ppermute | solution.py:492
  237.5 71.4 %collective-permute-start.53 = (bf16[4,4,2,96,768]{4,3,2,1,0:T(8,128)(2,1)}, bf16[4,4,2,96,768]{4,3,2,1,0:T(8,128)(2,1)}, u32[]{:S(2)}, u32[]{:S(2)}) collective-permute-start(bf16[4,4,2,96,768]{4,3,2,1,0:T(8,128)(2,1)} %get-tuple-element.44), channel_id=1, source_target_pairs={{0,4},{4,0},{8,12},{12,8},{16,20},{20,16},{24,28},{28,24},{1,5},{5... | collective-permute-start | bytes 14155784 | tf_op jit(solution)/shard_map/ppermute | solution.py:492
  291.5 27.5 %collective-permute-start.42 = (bf16[4,4,1,96,768]{4,3,1,0,2:T(8,128)(2,1)}, bf16[4,4,1,96,768]{4,3,1,0,2:T(8,128)(2,1)}, u32[]{:S(2)}, u32[]{:S(2)}) collective-permute-start(bf16[4,4,1,96,768]{4,3,1,0,2:T(8,128)(2,1)} %slice_bitcast_fusion), channel_id=1, source_target_pairs={{0,4},{4,0},{8,12},{12,8},{16,20},{20,16},{24,28},{28,24},{1,5},{5... | collective-permute-start | bytes 7077896 | tf_op jit(solution)/shard_map/ppermute | solution.py:492
  314.8 27.0 %collective-permute-start.54 = (bf16[4,2,96,768]{3,2,1,0:T(8,128)(2,1)S(1)}, bf16[4,2,96,768]{3,2,1,0:T(8,128)(2,1)S(1)}, u32[]{:S(2)}, u32[]{:S(2)}) collective-permute-start(bf16[4,2,96,768]{3,2,1,0:T(8,128)(2,1)S(1)} %get-tuple-element.79), channel_id=1, source_target_pairs={{0,8},{4,12},{8,0},{12,4},{16,24},{20,28},{24,16},{28,20},{1,9},{5... | collective-permute-start | bytes 3538952 | tf_op jit(solution)/shard_map/ppermute | solution.py:492
  314.9 27.9 %collective-permute-start.55 = (bf16[4,2,96,768]{3,2,1,0:T(8,128)(2,1)S(1)}, bf16[4,2,96,768]{3,2,1,0:T(8,128)(2,1)S(1)}, u32[]{:S(2)}, u32[]{:S(2)}) collective-permute-start(bf16[4,2,96,768]{3,2,1,0:T(8,128)(2,1)S(1)} %get-tuple-element.81), channel_id=1, source_target_pairs={{0,16},{4,20},{8,24},{12,28},{16,0},{20,4},{24,8},{28,12},{1,17},{... | collective-permute-start | bytes 3538952 | tf_op jit(solution)/shard_map/ppermute | solution.py:492
  315.2 51.1 %collective-permute-start.56 = (bf16[4,2,96,768]{3,2,1,0:T(8,128)(2,1)S(1)}, bf16[4,2,96,768]{3,2,1,0:T(8,128)(2,1)S(1)}, u32[]{:S(2)}, u32[]{:S(2)}) collective-permute-start(bf16[4,2,96,768]{3,2,1,0:T(8,128)(2,1)S(1)} %get-tuple-element.80), channel_id=1, source_target_pairs={{0,24},{4,28},{8,16},{12,20},{16,8},{20,12},{24,0},{28,4},{1,25},{... | collective-permute-start | bytes 3538952 | tf_op jit(solution)/shard_map/ppermute | solution.py:492
  317.6 93.1 %collective-permute-start.67 = (f32[12,768]{1,0:T(8,128)S(1)}, f32[12,768]{1,0:T(8,128)S(1)}, u32[]{:S(2)}, u32[]{:S(2)}) collective-permute-start(f32[12,768]{1,0:T(8,128)S(1)} %add_add_fusion.5), channel_id=1, source_target_pairs={{0,4},{4,0},{8,12},{12,8},{16,20},{20,16},{24,28},{28,24},{1,5},{5... | collective-permute-start | bytes 110600 | tf_op jit(solution)/shard_map/ppermute | solution.py:492
  319.1 98.5 %collective-permute-start.68 = (f32[12,768]{1,0:T(8,128)S(1)}, f32[12,768]{1,0:T(8,128)S(1)}, u32[]{:S(2)}, u32[]{:S(2)}) collective-permute-start(f32[12,768]{1,0:T(8,128)S(1)} %add_add_fusion.5), channel_id=1, source_target_pairs={{0,8},{4,12},{8,0},{12,4},{16,24},{20,28},{24,16},{28,20},{1,9},{5... | collective-permute-start | bytes 110600 | tf_op jit(solution)/shard_map/ppermute | solution.py:492
  341.8 39.0 %collective-permute-start.43 = (bf16[4,1,96,768]{3,2,0,1:T(8,128)(2,1)S(1)}, bf16[4,1,96,768]{3,2,0,1:T(8,128)(2,1)S(1)}, u32[]{:S(2)}, u32[]{:S(2)}) collective-permute-start(bf16[4,1,96,768]{3,2,0,1:T(8,128)(2,1)S(1)} %get-tuple-element.84), channel_id=1, source_target_pairs={{0,8},{4,12},{8,0},{12,4},{16,24},{20,28},{24,16},{28,20},{1,9},{5... | collective-permute-start | bytes 1769480 | tf_op jit(solution)/shard_map/ppermute | solution.py:492
  342.8 38.9 %collective-permute-start.44 = (bf16[4,1,96,768]{3,2,0,1:T(8,128)(2,1)S(1)}, bf16[4,1,96,768]{3,2,0,1:T(8,128)(2,1)S(1)}, u32[]{:S(2)}, u32[]{:S(2)}) collective-permute-start(bf16[4,1,96,768]{3,2,0,1:T(8,128)(2,1)S(1)} %get-tuple-element.85), channel_id=1, source_target_pairs={{0,16},{4,20},{8,24},{12,28},{16,0},{20,4},{24,8},{28,12},{1,17},{... | collective-permute-start | bytes 1769480 | tf_op jit(solution)/shard_map/ppermute | solution.py:492
  366.3 26.3 %collective-permute-start.45 = (bf16[4,1,96,768]{3,2,0,1:T(8,128)(2,1)S(1)}, bf16[4,1,96,768]{3,2,0,1:T(8,128)(2,1)S(1)}, u32[]{:S(2)}, u32[]{:S(2)}) collective-permute-start(bf16[4,1,96,768]{3,2,0,1:T(8,128)(2,1)S(1)} %slice_bitcast_fusion.6), channel_id=1, source_target_pairs={{0,24},{4,28},{8,16},{12,20},{16,8},{20,12},{24,0},{28,4},{1,25},{... | collective-permute-start | bytes 1769480 | tf_op jit(solution)/shard_map/ppermute | solution.py:492
  380.8 13.4 %collective-permute-start.57 = (bf16[2,96,768]{2,1,0:T(8,128)(2,1)S(1)}, bf16[2,96,768]{2,1,0:T(8,128)(2,1)S(1)}, u32[]{:S(2)}, u32[]{:S(2)}) collective-permute-start(bf16[2,96,768]{2,1,0:T(8,128)(2,1)S(1)} %get-tuple-element.117), channel_id=1, source_target_pairs={{0,1},{1,0},{2,3},{3,2},{4,5},{5,4},{6,7},{7,6},{8,9},{9,8},{10,11... | collective-permute-start | bytes 884744 | tf_op jit(solution)/shard_map/ppermute | solution.py:492
  381.8 17.3 %collective-permute-start.58 = (bf16[2,96,768]{2,1,0:T(8,128)(2,1)S(1)}, bf16[2,96,768]{2,1,0:T(8,128)(2,1)S(1)}, u32[]{:S(2)}, u32[]{:S(2)}) collective-permute-start(bf16[2,96,768]{2,1,0:T(8,128)(2,1)S(1)} %get-tuple-element.119), channel_id=1, source_target_pairs={{0,2},{1,3},{2,0},{3,1},{4,6},{5,7},{6,4},{7,5},{8,10},{9,11},{10,... | collective-permute-start | bytes 884744 | tf_op jit(solution)/shard_map/ppermute | solution.py:492
  392.6 17.7 %collective-permute-start.59 = (bf16[2,96,768]{2,1,0:T(8,128)(2,1)S(1)}, bf16[2,96,768]{2,1,0:T(8,128)(2,1)S(1)}, u32[]{:S(2)}, u32[]{:S(2)}) collective-permute-start(bf16[2,96,768]{2,1,0:T(8,128)(2,1)S(1)} %get-tuple-element.118), channel_id=1, source_target_pairs={{0,3},{1,2},{2,1},{3,0},{4,7},{5,6},{6,5},{7,4},{8,11},{9,10},{10,... | collective-permute-start | bytes 884744 | tf_op jit(solution)/shard_map/ppermute | solution.py:492
  394.2 23.4 %collective-permute-start.69 = (f32[12,768]{1,0:T(8,128)S(1)}, f32[12,768]{1,0:T(8,128)S(1)}, u32[]{:S(2)}, u32[]{:S(2)}) collective-permute-start(f32[12,768]{1,0:T(8,128)S(1)} %add_add_fusion.5), channel_id=1, source_target_pairs={{0,12},{4,8},{8,4},{12,0},{16,28},{20,24},{24,20},{28,16},{1,13},{... | collective-permute-start | bytes 110600 | tf_op jit(solution)/shard_map/ppermute | solution.py:492
  399.1 19.4 %collective-permute-start.70 = (f32[12,768]{1,0:T(8,128)S(1)}, f32[12,768]{1,0:T(8,128)S(1)}, u32[]{:S(2)}, u32[]{:S(2)}) collective-permute-start(f32[12,768]{1,0:T(8,128)S(1)} %add_add_fusion.5), channel_id=1, source_target_pairs={{0,16},{4,20},{8,24},{12,28},{16,0},{20,4},{24,8},{28,12},{1,17},{... | collective-permute-start | bytes 110600 | tf_op jit(solution)/shard_map/ppermute | solution.py:492
  417.5 14.9 %collective-permute-start.61 = (bf16[2,96,768]{2,1,0:T(8,128)(2,1)S(1)}, bf16[2,96,768]{2,1,0:T(8,128)(2,1)S(1)}, u32[]{:S(2)}, u32[]{:S(2)}) collective-permute-start(bf16[2,96,768]{2,1,0:T(8,128)(2,1)S(1)} %fusion.33), channel_id=1, source_target_pairs={{0,16},{4,20},{8,24},{12,28},{16,0},{20,4},{24,8},{28,12},{1,17},{... | collective-permute-start | bytes 884744 | tf_op jit(solution)/shard_map/ppermute | solution.py:492
  417.6 15.2 %collective-permute-start.62 = (bf16[2,96,768]{2,1,0:T(8,128)(2,1)S(1)}, bf16[2,96,768]{2,1,0:T(8,128)(2,1)S(1)}, u32[]{:S(2)}, u32[]{:S(2)}) collective-permute-start(bf16[2,96,768]{2,1,0:T(8,128)(2,1)S(1)} %fusion.33), channel_id=1, source_target_pairs={{0,24},{4,28},{8,16},{12,20},{16,8},{20,12},{24,0},{28,4},{1,25},{... | collective-permute-start | bytes 884744 | tf_op jit(solution)/shard_map/ppermute | solution.py:492
  418.5 21.2 %collective-permute-start.46 = (bf16[1,96,768]{2,1,0:T(8,128)(2,1)S(1)}, bf16[1,96,768]{2,1,0:T(8,128)(2,1)S(1)}, u32[]{:S(2)}, u32[]{:S(2)}) collective-permute-start(bf16[1,96,768]{2,1,0:T(8,128)(2,1)S(1)} %get-tuple-element.124), channel_id=1, source_target_pairs={{0,1},{1,0},{2,3},{3,2},{4,5},{5,4},{6,7},{7,6},{8,9},{9,8},{10,11... | collective-permute-start | bytes 442376 | tf_op jit(solution)/shard_map/ppermute | solution.py:492
  419.8 20.2 %collective-permute-start.47 = (bf16[1,96,768]{2,1,0:T(8,128)(2,1)S(1)}, bf16[1,96,768]{2,1,0:T(8,128)(2,1)S(1)}, u32[]{:S(2)}, u32[]{:S(2)}) collective-permute-start(bf16[1,96,768]{2,1,0:T(8,128)(2,1)S(1)} %get-tuple-element.125), channel_id=1, source_target_pairs={{0,2},{1,3},{2,0},{3,1},{4,6},{5,7},{6,4},{7,5},{8,10},{9,11},{10,... | collective-permute-start | bytes 442376 | tf_op jit(solution)/shard_map/ppermute | solution.py:492
  421.0 19.5 %collective-permute-start.48 = (bf16[1,96,768]{2,1,0:T(8,128)(2,1)S(1)}, bf16[1,96,768]{2,1,0:T(8,128)(2,1)S(1)}, u32[]{:S(2)}, u32[]{:S(2)}) collective-permute-start(bf16[1,96,768]{2,1,0:T(8,128)(2,1)S(1)} %slice_bitcast_fusion.14), channel_id=1, source_target_pairs={{0,3},{1,2},{2,1},{3,0},{4,7},{5,6},{6,5},{7,4},{8,11},{9,10},{10,... | collective-permute-start | bytes 442376 | tf_op jit(solution)/shard_map/ppermute | solution.py:492
  440.6 66.7 %collective-permute-start.63 = (bf16[4,2,96,768]{3,2,1,0:T(8,128)(2,1)S(1)}, bf16[4,2,96,768]{3,2,1,0:T(8,128)(2,1)S(1)}, u32[]{:S(2)}, u32[]{:S(2)}) collective-permute-start(bf16[4,2,96,768]{3,2,1,0:T(8,128)(2,1)S(1)} %get-tuple-element.116), channel_id=1, source_target_pairs={{0,4},{4,0},{8,12},{12,8},{16,20},{20,16},{24,28},{28,24},{1,5},{5... | collective-permute-start | bytes 3538952 | tf_op jit(solution)/shard_map/ppermute | solution.py:492
  441.2 22.9 %collective-permute-start.39 = (bf16[128,768]{1,0:T(8,128)(2,1)S(1)}, bf16[128,768]{1,0:T(8,128)(2,1)S(1)}, u32[]{:S(2)}, u32[]{:S(2)}) collective-permute-start(bf16[128,768]{1,0:T(8,128)(2,1)S(1)} %get-tuple-element.89), channel_id=1, source_target_pairs={{0,20},{4,16},{8,28},{12,24},{16,4},{20,0},{24,12},{28,8},{1,21},{... | collective-permute-start | bytes 589832 | tf_op jit(solution)/shard_map/ppermute | solution.py:492
  450.0 12.9 %collective-permute-start.50 = (bf16[1,96,768]{2,1,0:T(8,128)(2,1)S(1)}, bf16[1,96,768]{2,1,0:T(8,128)(2,1)S(1)}, u32[]{:S(2)}, u32[]{:S(2)}) collective-permute-start(bf16[1,96,768]{2,1,0:T(8,128)(2,1)S(1)} %fusion.35), channel_id=1, source_target_pairs={{0,16},{4,20},{8,24},{12,28},{16,0},{20,4},{24,8},{28,12},{1,17},{... | collective-permute-start | bytes 442376 | tf_op jit(solution)/shard_map/ppermute | solution.py:492
  464.1 32.1 %collective-permute-start.52 = (bf16[4,1,96,768]{3,2,1,0:T(8,128)(2,1)S(1)}, bf16[4,1,96,768]{3,2,1,0:T(8,128)(2,1)S(1)}, u32[]{:S(2)}, u32[]{:S(2)}) collective-permute-start(bf16[4,1,96,768]{3,2,1,0:T(8,128)(2,1)S(1)} %get-tuple-element.123), channel_id=1, source_target_pairs={{0,4},{4,0},{8,12},{12,8},{16,20},{20,16},{24,28},{28,24},{1,5},{5... | collective-permute-start | bytes 1769480 | tf_op jit(solution)/shard_map/ppermute | solution.py:492
  475.3 15.9 %collective-permute-start.32 = (bf16[128,768]{1,0:T(8,128)(2,1)S(1)}, bf16[128,768]{1,0:T(8,128)(2,1)S(1)}, u32[]{:S(2)}, u32[]{:S(2)}) collective-permute-start(bf16[128,768]{1,0:T(8,128)(2,1)S(1)} %get-tuple-element.96), channel_id=1, source_target_pairs={{0,20},{4,16},{8,28},{12,24},{16,4},{20,0},{24,12},{28,8},{1,21},{... | collective-permute-start | bytes 589832 | tf_op jit(solution)/shard_map/ppermute | solution.py:492
  (83 other events, 960.0 us)
